TPU v7x, 32 devices: a whole 2x2x4 slice. The times are simulated.
32 devices in a mesh: expert: 8 (over y, x, core), dp: 4 (over z).
Axes of the slice: x: 2, y: 2, z: 4, core: 2. Of those that a mesh axis runs over, the one named last changes fastest.
Arguments:
- tokens: bfloat16 [4096, 2048], P(('expert', 'dp')), may hold values from -6 to 6
- routes: int32 [4096, 2], P(('expert', 'dp')), may hold values from 0 to 31, all different within a row; in each aligned block of 128 rows (0 to 127, 128 to 255, ...) at most 16 rows name the same one
- gate_probs: float32 [4096, 2], P(('expert', 'dp')), may hold values from 0.05 to 1
- norm_gain: float32 [2048], replicated, may hold values from 0.1 to 1.9
- w_gate: bfloat16 [32, 2048, 768], P(('expert', 'dp')), may hold values from -0.125 to 0.125
- w_up: bfloat16 [32, 2048, 768], P(('expert', 'dp')), may hold values from -0.125 to 0.125
- w_down: bfloat16 [32, 768, 2048], P(('expert', 'dp')), may hold values from -0.21875 to 0.21875
- out_grad: bfloat16 [4096, 2048], P(('expert', 'dp')), may hold values from -6 to 6
Outputs:
- mixed: bfloat16 [4096, 2048], P(('expert', 'dp'))
- grad_probs: float32 [4096, 2], P(('expert', 'dp'))
- grad_gain: float32 [2048], replicated
- grad_tokens: bfloat16 [4096, 2048], P(('expert', 'dp'))
- grad_gate: bfloat16 [32, 2048, 768], P(('expert', 'dp'))
- grad_up: bfloat16 [32, 2048, 768], P(('expert', 'dp'))
- grad_down: bfloat16 [32, 768, 2048], P(('expert', 'dp'))
Inputs may be any that keep to these rules, and one draw needn't show every extreme that they name: `routes`: each row names 2 different experts. Among the 128 rows of one device no expert is named more than 16 times, a bound that some block reaches.
All inputs are finite; a program needn't handle non-finite values.
Results may differ from a plain program's by a relative error of at most 0.0072.
Values may be sent and summed in bfloat16 or wider, within the bound.
A program may use at most 128 MiB of HBM per device.

v0:
```python
import jax
import jax.numpy as jnp
from jax import lax
from jax.sharding import PartitionSpec as P


def outward(rows, capacity):
    width = rows.shape[-1]
    shaped = rows.reshape(lax.axis_size(("expert", "dp")), capacity, width)
    moved = lax.all_to_all(shaped, ("expert", "dp"), split_axis=0, concat_axis=0, tiled=True)
    return moved.reshape(rows.shape)


def inward(rows, capacity):
    width = rows.shape[-1]
    shaped = rows.reshape(lax.axis_size(("expert", "dp")), capacity, width)
    moved = lax.all_to_all(shaped, ("expert", "dp"), split_axis=0, concat_axis=0, tiled=True)
    return moved.reshape(rows.shape)


def contract(left, right, left_dim, right_dim):
    return lax.dot_general(
        left, right, (((left_dim,), (right_dim,)), ((), ())), preferred_element_type=jnp.float32
    )


def forward_expert(arrived, gate_matrix, up_matrix, down_matrix):
    pre_gate = jnp.dot(arrived, gate_matrix, preferred_element_type=jnp.float32)
    up_value = jnp.dot(arrived, up_matrix, preferred_element_type=jnp.float32)
    sigmoid_gate = jax.nn.sigmoid(pre_gate)
    activated = pre_gate * sigmoid_gate
    hidden = (activated * up_value).astype(jnp.bfloat16)
    expert_out = jnp.dot(hidden, down_matrix, preferred_element_type=jnp.float32).astype(
        jnp.bfloat16
    )
    return (pre_gate, up_value, sigmoid_gate, activated, hidden, expert_out)


def backward_expert(arrived, arrived_grad, saved, gate_matrix, up_matrix, down_matrix):
    pre_gate, up_value, sigmoid_gate, activated, hidden = saved
    grad_hidden = contract(arrived_grad, down_matrix, 1, 1)
    grad_down = contract(hidden, arrived_grad, 0, 0).astype(jnp.bfloat16)
    grad_pre = (
        grad_hidden * up_value * sigmoid_gate * (1.0 + pre_gate * (1.0 - sigmoid_gate))
    ).astype(jnp.bfloat16)
    grad_upval = (grad_hidden * activated).astype(jnp.bfloat16)
    grad_back = (
        contract(grad_pre, gate_matrix, 1, 1) + contract(grad_upval, up_matrix, 1, 1)
    ).astype(jnp.bfloat16)
    grad_gate = contract(arrived, grad_pre, 0, 0).astype(jnp.bfloat16)
    grad_up = contract(arrived, grad_upval, 0, 0).astype(jnp.bfloat16)
    return (grad_back, grad_gate, grad_up, grad_down)


def on_device(tokens, routes, gate_probs, norm_gain, w_gate, w_up, w_down, out_grad):
    devices_all = lax.axis_size(("expert", "dp"))
    tok_rows, width = tokens.shape
    top_count = routes.shape[1]
    assigned = tok_rows * top_count
    capacity = 2 * assigned // devices_all
    inputs = tokens.astype(jnp.float32)
    inverse_rms = lax.rsqrt(jnp.mean(inputs * inputs, axis=1, keepdims=True) + 1e-06)
    normed = inputs * inverse_rms
    scaled = (normed * norm_gain).astype(jnp.bfloat16)
    flat_ids = routes.reshape(assigned)
    onehot = (flat_ids[:, None] == jnp.arange(devices_all, dtype=jnp.int32)[None, :]).astype(
        jnp.int32
    )
    earlier = jnp.cumsum(onehot, axis=0) - onehot
    slot_index = flat_ids * capacity + jnp.sum(earlier * onehot, axis=1)
    gate_matrix = w_gate[0]
    up_matrix = w_up[0]
    down_matrix = w_down[0]
    weights = gate_probs[:, :, None]
    grad_in = out_grad.astype(jnp.float32)
    grad_rows = (weights * grad_in[:, None, :]).astype(jnp.bfloat16).reshape(assigned, width)
    repeated = jnp.repeat(scaled, top_count, axis=0)
    empty = jnp.zeros((devices_all * capacity, width), jnp.bfloat16)
    arrived = outward(empty.at[slot_index].set(repeated), capacity)
    pre_gate, up_value, sigmoid_gate, activated, hidden, expert_out = forward_expert(
        arrived, gate_matrix, up_matrix, down_matrix
    )
    returned = inward(expert_out, capacity)
    picked = returned[slot_index].reshape(tok_rows, top_count, width).astype(jnp.float32)
    arrived_grad = outward(empty.at[slot_index].set(grad_rows), capacity)
    grad_back, grad_gate, grad_up, grad_down = backward_expert(
        arrived,
        arrived_grad,
        (pre_gate, up_value, sigmoid_gate, activated, hidden),
        gate_matrix,
        up_matrix,
        down_matrix,
    )
    returned_grad = inward(grad_back, capacity)
    grad_normed = jnp.sum(
        returned_grad[slot_index].reshape(tok_rows, top_count, width).astype(jnp.float32), axis=1
    )
    mixed = (inputs + jnp.sum(weights * picked, axis=1)).astype(jnp.bfloat16)
    grad_probs = jnp.sum(grad_in[:, None, :] * picked, axis=2)
    gain_part = jnp.sum(grad_normed * normed, axis=0)
    grad_gain = lax.psum(gain_part, ("expert", "dp"))
    grad_scaled = grad_normed * norm_gain
    grad_tokens = (
        grad_in
        + inverse_rms
        * (grad_scaled - normed * jnp.mean(grad_scaled * normed, axis=1, keepdims=True))
    ).astype(jnp.bfloat16)
    return (
        mixed,
        grad_probs,
        grad_gain,
        grad_tokens,
        grad_gate[None],
        grad_up[None],
        grad_down[None],
    )


def solution(mesh):
    return jax.shard_map(
        on_device,
        mesh=mesh,
        in_specs=(
            P(("expert", "dp"), None),
            P(("expert", "dp"), None),
            P(("expert", "dp"), None),
            P(),
            P(("expert", "dp"), None, None),
            P(("expert", "dp"), None, None),
            P(("expert", "dp"), None, None),
            P(("expert", "dp"), None),
        ),
        out_specs=(
            P(("expert", "dp"), None),
            P(("expert", "dp"), None),
            P(),
            P(("expert", "dp"), None),
            P(("expert", "dp"), None, None),
            P(("expert", "dp"), None, None),
            P(("expert", "dp"), None, None),
        ),
        check_vma=False,
    )
```

profile of v0, /device:TPU:0, one launch (start us, length us, event | category | flops | bytes accessed | tf_op | source)
XLA Modules:
  0.0 298.9 jit_solution(12713489355815801809)
XLA Ops:
  0.6 0.0 copy-start
  0.6 0.9 copy.24
  1.6 0.1 eq.29
  1.7 0.1 eq.25
  1.9 0.7 broadcast_multiply_fusion
  2.6 0.6 reduce-window.6
  3.1 0.2 slice_reduce_fusion
  3.4 0.1 copy.23
  3.5 0.1 mul.124
  3.6 1.2 fusion.32
  4.9 1.2 fusion.25
  6.1 1.6 broadcast_in_dim.11
  7.7 2.2 reshape.153
  10.0 0.1 fusion.41
  10.1 4.4 %scatter_custom_fusion = bf16[512,2048]{1,0:T(8,128)(2,1)} fusion(s32[256]{0:T(256)S(1)} %bitcast.72, bf16[256,2048]{1,0:T(8,128)(2,1)} %reshape.153, bf16[]{:T(256)} %constant.8.clone.1), kind=kCustom, calls=%fused_computation.51 | custom fusion | bytes 2097664 | tf_op jit(solution)/shard_map/scatter | solution.py:79
  14.5 0.0 copy-start.2
  14.5 7.4 %all-to-all-start = ((bf16[32,16,2048]{2,1,0:T(8,128)(2,1)}), bf16[32,16,2048]{2,1,0:T(8,128)(2,1)}, u32[]{:S(2)}, u32[]{:S(2)}) async-start(bf16[32,16,2048]{2,1,0:T(8,128)(2,1)} %bitcast.69), calls=%async_computation | async-start | bytes 4194304 | tf_op jit(solution)/shard_map/all_to_all | solution.py:10
  21.9 0.0 copy-done.2
  21.9 0.1 copy.22
  22.0 0.1 mul.136
  22.2 3.4 %mul.134 = f32[128,2,2048]{2,1,0:T(2,128)} broadcast(bf16[128,2048]{1,0:T(8,128)(2,1)} %param.15), dimensions={0,2} | broadcast | bytes 2621440 | tf_op jit(solution)/shard_map/mul | solution.py:99
  25.6 3.6 %mul.138 = f32[256,2048]{1,0:T(8,128)} reshape(f32[128,2,2048]{2,1,0:T(2,128)} %mul.134) | data formatting | bytes 4194304 | tf_op jit(solution)/shard_map/mul | solution.py:99
  29.2 4.8 %scatter_custom_fusion.1 = bf16[512,2048]{1,0:T(8,128)(2,1)} fusion(s32[256]{0:T(256)S(1)} %bitcast.73, f32[256,2048]{1,0:T(8,128)} %mul.138, f32[256]{0:T(256)S(1)} %mul.136, bf16[]{:T(256)} %constant.8.clone.1), kind=kCustom, calls=%fused_computation.48 | custom fusion | flops 1048576 | bytes 4195330 | tf_op jit(solution)/shard_map/scatter | solution.py:85
  34.1 35.3 %all-to-all-done = bf16[32,16,2048]{2,1,0:T(8,128)(2,1)} async-done(((bf16[32,16,2048]{2,1,0:T(8,128)(2,1)}), bf16[32,16,2048]{2,1,0:T(8,128)(2,1)}, u32[]{:S(2)}, u32[]{:S(2)}) %all-to-all-start) | async-done | bytes 2097184 | tf_op jit(solution)/shard_map/all_to_all | solution.py:10
  69.4 4.5 %all-to-all-start.2 = ((bf16[32,16,2048]{2,1,0:T(8,128)(2,1)}), bf16[32,16,2048]{2,1,0:T(8,128)(2,1)}, u32[]{:S(2)}, u32[]{:S(2)}) async-start(bf16[32,16,2048]{2,1,0:T(8,128)(2,1)} %bitcast.68), calls=%async_computation.2 | async-start | bytes 4194304 | tf_op jit(solution)/shard_map/all_to_all | solution.py:10
  73.9 5.5 %fusion.6 = f32[512,768]{1,0:T(8,128)} fusion(bf16[512,2048]{1,0:T(8,128)(2,1)} %bitcast.4, bf16[1,2048,768]{2,1,0:T(8,128)(2,1)} %param.13), kind=kOutput, calls=%fused_computation.14 | convolution fusion | flops 1610612736 | bytes 6815744 | tf_op jit(solution)/shard_map/dot_general | solution.py:29
  79.3 41.4 %all-to-all-done.2 = bf16[32,16,2048]{2,1,0:T(8,128)(2,1)} async-done(((bf16[32,16,2048]{2,1,0:T(8,128)(2,1)}), bf16[32,16,2048]{2,1,0:T(8,128)(2,1)}, u32[]{:S(2)}, u32[]{:S(2)}) %all-to-all-start.2) | async-done | bytes 2097184 | tf_op jit(solution)/shard_map/all_to_all | solution.py:10
  120.7 0.0 copy-start.8
  120.7 4.5 %fusion = f32[512,768]{1,0:T(8,128)S(1)} fusion(bf16[512,2048]{1,0:T(8,128)(2,1)} %bitcast.11, bf16[1,768,2048]{2,1,0:T(8,128)(2,1)} %param.14), kind=kOutput, calls=%fused_computation.8 | convolution fusion | flops 1610612736 | bytes 6815744 | tf_op jit(solution)/shard_map/dot_general | solution.py:22
  125.2 0.0 copy-done
  125.2 0.0 copy-done.8
  125.2 0.0 copy-start.3
  125.2 5.0 %multiply_convert_fusion.2 = (bf16[512,768]{1,0:T(8,128)(2,1)S(1)}, bf16[512,768]{1,0:T(8,128)(2,1)S(1)}, bf16[512,768]{1,0:T(8,128)(2,1)}) fusion(f32[512,768]{1,0:T(8,128)S(1)} %fusion, f32[512,768]{1,0:T(8,128)S(1)} %copy-done.8, bf16[512,2048]{1,0:T(8,128)(2,1)} %bitcast.4, bf16[1,2048,768]{2,1,0:T(8,128)(2,1)S(1)} %copy-done), kind=kOutput, calls=%fused_computation.28 | convolution fusion | flops 1616510976 | bytes 10747904 | tf_op jit(solution)/shard_map/dot_general | solution.py:28
  130.2 0.0 copy-start.5
  130.2 0.0 copy-start.4
  130.2 0.0 copy-done.3
  130.2 1.8 fusion.4
  132.0 0.0 copy-done.5
  132.0 0.0 copy-done.4
  132.0 3.2 %add_convert_fusion = bf16[512,2048]{1,0:T(8,128)(2,1)} fusion(f32[512,2048]{1,0:T(8,128)S(1)} %fusion.4, bf16[512,768]{1,0:T(8,128)(2,1)S(1)} %get-tuple-element.18, bf16[1,2048,768]{2,1,0:T(8,128)(2,1)S(1)} %copy-done), kind=kOutput, calls=%fused_computation.4 | convolution fusion | flops 1612709888 | bytes 10223616 | tf_op jit(solution)/shard_map/dot_general | solution.py:22
  135.2 4.7 %all-to-all-start.3 = ((bf16[32,16,2048]{2,1,0:T(8,128)(2,1)}), bf16[32,16,2048]{2,1,0:T(8,128)(2,1)}, u32[]{:S(2)}, u32[]{:S(2)}) async-start(bf16[32,16,2048]{2,1,0:T(8,128)(2,1)} %bitcast.71), calls=%async_computation.3 | async-start | bytes 4194304 | tf_op jit(solution)/shard_map/all_to_all | solution.py:17
  139.9 5.2 %fusion.12 = bf16[512,2048]{1,0:T(8,128)(2,1)} fusion(bf16[512,768]{1,0:T(8,128)(2,1)} %get-tuple-element.20, bf16[1,768,2048]{2,1,0:T(8,128)(2,1)} %param.14), kind=kOutput, calls=%fused_computation.20 | convolution fusion | flops 1611661312 | bytes 6029312 | tf_op jit(solution)/shard_map/dot_general | solution.py:33
  145.2 42.1 %all-to-all-done.3 = bf16[32,16,2048]{2,1,0:T(8,128)(2,1)} async-done(((bf16[32,16,2048]{2,1,0:T(8,128)(2,1)}), bf16[32,16,2048]{2,1,0:T(8,128)(2,1)}, u32[]{:S(2)}, u32[]{:S(2)}) %all-to-all-start.3) | async-done | bytes 2097184 | tf_op jit(solution)/shard_map/all_to_all | solution.py:17
  187.2 4.7 %all-to-all-start.1 = ((bf16[32,16,2048]{2,1,0:T(8,128)(2,1)}), bf16[32,16,2048]{2,1,0:T(8,128)(2,1)}, u32[]{:S(2)}, u32[]{:S(2)}) async-start(bf16[32,16,2048]{2,1,0:T(8,128)(2,1)} %bitcast.70), calls=%async_computation.1 | async-start | bytes 4194304 | tf_op jit(solution)/shard_map/all_to_all | solution.py:17
  191.9 2.1 convert_element_type.75
  194.1 0.0 copy-start.6
  194.1 5.3 %fusion.15 = bf16[1,2048,768]{2,1,0:T(8,128)(2,1)} fusion(bf16[512,2048]{1,0:T(8,128)(2,1)} %bitcast.4, bf16[512,768]{1,0:T(8,128)(2,1)} %copy-done.4), kind=kOutput, calls=%fused_computation.21 | convolution fusion | flops 1612185600 | bytes 6029312 | tf_op jit(solution)/shard_map/dot_general | solution.py:22
  199.4 0.0 copy-done.6
  199.4 0.0 copy-start.7
  199.4 5.2 %fusion.16 = bf16[1,2048,768]{2,1,0:T(8,128)(2,1)} fusion(bf16[512,2048]{1,0:T(8,128)(2,1)} %bitcast.4, bf16[512,768]{1,0:T(8,128)(2,1)S(1)} %copy-done.6), kind=kOutput, calls=%fused_computation.22 | convolution fusion | flops 1612185600 | bytes 6029312 | tf_op jit(solution)/shard_map/dot_general | solution.py:22
  204.6 0.0 copy-done.7
  204.6 5.1 %fusion.17 = bf16[1,768,2048]{2,1,0:T(8,128)(2,1)} fusion(bf16[512,768]{1,0:T(8,128)(2,1)S(1)} %copy-done.7, bf16[512,2048]{1,0:T(8,128)(2,1)} %bitcast.11), kind=kOutput, calls=%fused_computation.23 | convolution fusion | flops 1612185600 | bytes 6029312 | tf_op jit(solution)/shard_map/dot_general | solution.py:22
  209.7 5.2 %gather_fusion.1 = bf16[256,2048]{1,0:T(8,128)(2,1)} fusion(bf16[512,2048]{1,0:T(8,128)(2,1)} %bitcast.13, s32[1024]{0:T(1024)S(1)} %pad_clamp_fusion), kind=kCustom, calls=%fused_computation.1 | custom fusion | bytes 2098176 | tf_op jit(solution)/shard_map/gather | solution.py:96
  214.9 3.4 %reshape.132 = f32[128,2,2048]{2,1,0:T(2,128)} reshape(bf16[256,2048]{1,0:T(8,128)(2,1)} %gather_fusion.1) | data formatting | bytes 3145728 | tf_op jit(solution)/shard_map/convert_element_type | solution.py:96
  218.3 5.1 %reduce_sum.70 = f32[128,2048]{1,0:T(8,128)} reduce(f32[128,2,2048]{2,1,0:T(2,128)} %reshape.132, f32[]{:T(128)} %constant.7.clone.1), dimensions={1}, to_apply=%region_8.9 | reduce | flops 262144 | bytes 3145732 | tf_op jit(solution)/shard_map/reduce_sum | solution.py:95
  223.4 0.0 copy-done.1
  223.4 1.8 fusion.27
  225.2 13.5 %all-to-all-done.1 = bf16[32,16,2048]{2,1,0:T(8,128)(2,1)} async-done(((bf16[32,16,2048]{2,1,0:T(8,128)(2,1)}), bf16[32,16,2048]{2,1,0:T(8,128)(2,1)}, u32[]{:S(2)}, u32[]{:S(2)}) %all-to-all-start.1) | async-done | bytes 2097184 | tf_op jit(solution)/shard_map/all_to_all | solution.py:17
  238.7 5.2 %gather_fusion = bf16[256,2048]{1,0:T(8,128)(2,1)} fusion(bf16[512,2048]{1,0:T(8,128)(2,1)} %bitcast.9, s32[1024]{0:T(1024)S(1)} %pad_clamp_fusion), kind=kCustom, calls=%fused_computation | custom fusion | bytes 2098176 | tf_op jit(solution)/shard_map/gather | solution.py:84
  243.9 3.4 %reshape.131 = f32[128,2,2048]{2,1,0:T(2,128)} reshape(bf16[256,2048]{1,0:T(8,128)(2,1)} %gather_fusion) | data formatting | bytes 3145728 | tf_op jit(solution)/shard_map/convert_element_type | solution.py:84
  247.3 41.3 %psum.7 = f32[2048]{0:T(1024)} all-reduce(f32[2048]{0:T(1024)S(1)} %get-tuple-element.17), channel_id=1, replica_groups=mesh['expert'=8,'dp'=4] {'expert','dp'}, use_global_device_ids=true, to_apply=%region_10.11 | all-reduce | flops 2048 | bytes 16384 | tf_op jit(solution)/shard_map/psum | solution.py:101
  288.6 6.4 %multiply_reduce_fusion = (f32[128,2]{1,0:T(8,128)S(1)}, f32[128,2048]{1,0:T(8,128)}) fusion(f32[128,2,2048]{2,1,0:T(2,128)} %reshape.131, f32[128,2048]{1,0:T(8,128)} %convert_element_type.75, f32[128,2]{1,0:T(8,128)S(1)} %copy.22), kind=kLoop, calls=%fused_computation.25 | loop fusion | flops 1834752 | bytes 4196352 | tf_op jit(solution)/shard_map/reduce_sum | solution.py:99
  295.0 0.6 copy.28
  295.7 3.3 %fusion.31 = (bf16[128,2048]{1,0:T(8,128)(2,1)}, bf16[128,2048]{1,0:T(8,128)(2,1)}) fusion(bf16[128,2048]{1,0:T(8,128)(2,1)} %param.8, f32[128,2048]{1,0:T(8,128)} %reduce_sum.70, f32[128]{0:T(128)S(1)} %broadcast_multiply_fusion.1, f32[2048]{0:T(1024)S(1)} %copy-done.1, f32[128]{0:T(128)S(1)} %add_rsqrt_fusion, bf16[128,2048]{1,0:T(8,128)(2,1)} %param.15, ...), kind=kLoop, calls=%fused_computation.45 | loop fusion | flops 2883584 | bytes 4203520 | tf_op jit(solution)/shard_map/convert_element_type | solution.py:107
  (8 shorter events, 0.1 us)
Async XLA Ops:
  0.6 124.6 %copy-start = (bf16[1,2048,768]{2,1,0:T(8,128)(2,1)S(1)}, bf16[1,2048,768]{2,1,0:T(8,128)(2,1)}, u32[]{:S(2)}) copy-start(bf16[1,2048,768]{2,1,0:T(8,128)(2,1)} %param.12) | copy-start | bytes 9437188
  14.5 7.4 %copy-start.2 = (f32[128,2]{0,1:T(2,128)S(1)}, f32[128,2]{0,1:T(2,128)}, u32[]{:S(2)}) copy-start(f32[128,2]{0,1:T(2,128)} %param.10) | copy-start | bytes 3076
  14.5 54.9 %all-to-all-start = ((bf16[32,16,2048]{2,1,0:T(8,128)(2,1)}), bf16[32,16,2048]{2,1,0:T(8,128)(2,1)}, u32[]{:S(2)}, u32[]{:S(2)}) async-start(bf16[32,16,2048]{2,1,0:T(8,128)(2,1)} %bitcast.69), calls=%async_computation | async-start | bytes 4194304 | tf_op jit(solution)/shard_map/all_to_all | solution.py:10
  69.4 51.3 %all-to-all-start.2 = ((bf16[32,16,2048]{2,1,0:T(8,128)(2,1)}), bf16[32,16,2048]{2,1,0:T(8,128)(2,1)}, u32[]{:S(2)}, u32[]{:S(2)}) async-start(bf16[32,16,2048]{2,1,0:T(8,128)(2,1)} %bitcast.68), calls=%async_computation.2 | async-start | bytes 4194304 | tf_op jit(solution)/shard_map/all_to_all | solution.py:10
  120.7 4.5 %copy-start.8 = (f32[512,768]{1,0:T(8,128)S(1)}, f32[512,768]{1,0:T(8,128)}, u32[]{:S(2)}) copy-start(f32[512,768]{1,0:T(8,128)} %fusion.6) | copy-start | bytes 4718596
  125.2 5.0 %copy-start.3 = (bf16[1,2048,768]{2,1,0:T(8,128)(2,1)S(1)}, bf16[1,2048,768]{2,1,0:T(8,128)(2,1)}, u32[]{:S(2)}) copy-start(bf16[1,2048,768]{2,1,0:T(8,128)(2,1)} %param.13) | copy-start | bytes 9437188
  130.2 1.8 copy-start.5
  130.2 1.8 copy-start.4
  135.2 52.0 %all-to-all-start.3 = ((bf16[32,16,2048]{2,1,0:T(8,128)(2,1)}), bf16[32,16,2048]{2,1,0:T(8,128)(2,1)}, u32[]{:S(2)}, u32[]{:S(2)}) async-start(bf16[32,16,2048]{2,1,0:T(8,128)(2,1)} %bitcast.71), calls=%async_computation.3 | async-start | bytes 4194304 | tf_op jit(solution)/shard_map/all_to_all | solution.py:17
  187.2 51.4 %all-to-all-start.1 = ((bf16[32,16,2048]{2,1,0:T(8,128)(2,1)}), bf16[32,16,2048]{2,1,0:T(8,128)(2,1)}, u32[]{:S(2)}, u32[]{:S(2)}) async-start(bf16[32,16,2048]{2,1,0:T(8,128)(2,1)} %bitcast.70), calls=%async_computation.1 | async-start | bytes 4194304 | tf_op jit(solution)/shard_map/all_to_all | solution.py:17
  194.1 5.3 %copy-start.6 = (bf16[512,768]{1,0:T(8,128)(2,1)S(1)}, bf16[512,768]{1,0:T(8,128)(2,1)}, u32[]{:S(2)}) copy-start(bf16[512,768]{1,0:T(8,128)(2,1)} %copy-done.5) | copy-start | bytes 2359300
  199.4 5.2 %copy-start.7 = (bf16[512,768]{1,0:T(8,128)(2,1)S(1)}, bf16[512,768]{1,0:T(8,128)(2,1)}, u32[]{:S(2)}) copy-start(bf16[512,768]{1,0:T(8,128)(2,1)} %get-tuple-element.20) | copy-start | bytes 2359300
  218.3 5.1 %copy-start.1 = (f32[2048]{0:T(1024)S(1)}, f32[2048]{0:T(1024)}, u32[]{:S(2)}) copy-start(f32[2048]{0:T(1024)} %param.11) | copy-start | bytes 24580
where the time goes:
time: 300 us; the launch traced here: 299 us
  waiting for transfers between devices  132 us (44%)
  blocking collectives  41.3 us (14%)
  matrix products  40.7 us (14%)
  local copies, waits for them, and re-layouts  35.1 us (12%)
  other arithmetic  27.4 us (9%)
  starting transfers between devices  21.3 us (7%)
    all_to_all x2, waiting for transfers between devices, outward(): lax.all_to_all(shaped, ('expert', 'dp'), split_axis=0, concat_axis=0, til...  76.7 us
    all_to_all x2, waiting for transfers between devices, inward(): lax.all_to_all(shaped, ('expert', 'dp'), split_axis=0, concat_axis=0, til...  55.6 us
    psum x1, blocking collectives, on_device(): grad_gain = lax.psum(gain_part, ('expert', 'dp'))  41.3 us
    dot_general x6, matrix products, contract(): lax.dot_general(left, right, (((left_dim,), (right_dim,)), ((), ())), pre...  25 us
    all_to_all x2, starting transfers between devices, outward(): lax.all_to_all(shaped, ('expert', 'dp'), split_axis=0, concat_axis=0, til...  11.9 us
    all_to_all x2, starting transfers between devices, inward(): lax.all_to_all(shaped, ('expert', 'dp'), split_axis=0, concat_axis=0, til...  9.4 us
    mul x2, local copies, waits for them, and re-layouts, on_device(): grad_probs = jnp.sum(grad_in[:, None, :] * picked, axis=2)  7.06 us
    reduce_sum x1, other arithmetic, on_device(): grad_probs = jnp.sum(grad_in[:, None, :] * picked, axis=2)  6.41 us
  transfers between devices with their start and end apart: 4, of which 4 were waited for; matrix products, arithmetic and copies ran while one was open for 19% of the time, Pallas kernels for 0%

commit v1 on v0

--- a/solution.py
+++ b/solution.py
@@ -63,11 +63,11 @@
     normed = inputs * inverse_rms
     scaled = (normed * norm_gain).astype(jnp.bfloat16)
     flat_ids = routes.reshape(assigned)
-    onehot = (flat_ids[:, None] == jnp.arange(devices_all, dtype=jnp.int32)[None, :]).astype(
-        jnp.int32
-    )
-    earlier = jnp.cumsum(onehot, axis=0) - onehot
-    slot_index = flat_ids * capacity + jnp.sum(earlier * onehot, axis=1)
+    places = jnp.arange(assigned, dtype=jnp.int32)
+    same = flat_ids[:, None] == flat_ids[None, :]
+    before = places[None, :] < places[:, None]
+    rank = jnp.sum((same & before).astype(jnp.int32), axis=1)
+    slot_index = flat_ids * capacity + rank
     gate_matrix = w_gate[0]
     up_matrix = w_up[0]
     down_matrix = w_down[0]

time: 300 us -> 299 us (level)
  no operation moved by 1% of the time
where the time goes in v1:
time: 299 us; the launch traced here: 298 us
  waiting for transfers between devices  132 us (44%)
  blocking collectives  41.3 us (14%)
  matrix products  40.7 us (14%)
  local copies, waits for them, and re-layouts  34.8 us (12%)
  other arithmetic  26.9 us (9%)
  starting transfers between devices  21.3 us (7%)
    all_to_all x2, waiting for transfers between devices, outward(): lax.all_to_all(shaped, ('expert', 'dp'), split_axis=0, concat_axis=0, til...  76.7 us
    all_to_all x2, waiting for transfers between devices, inward(): lax.all_to_all(shaped, ('expert', 'dp'), split_axis=0, concat_axis=0, til...  55.6 us
    psum x1, blocking collectives, on_device(): grad_gain = lax.psum(gain_part, ('expert', 'dp'))  41.3 us
    dot_general x6, matrix products, contract(): lax.dot_general(left, right, (((left_dim,), (right_dim,)), ((), ())), pre...  25 us
    all_to_all x2, starting transfers between devices, outward(): lax.all_to_all(shaped, ('expert', 'dp'), split_axis=0, concat_axis=0, til...  11.9 us
    all_to_all x2, starting transfers between devices, inward(): lax.all_to_all(shaped, ('expert', 'dp'), split_axis=0, concat_axis=0, til...  9.41 us
    mul x2, local copies, waits for them, and re-layouts, on_device(): grad_probs = jnp.sum(grad_in[:, None, :] * picked, axis=2)  7.06 us
    reduce_sum x1, other arithmetic, on_device(): grad_probs = jnp.sum(grad_in[:, None, :] * picked, axis=2)  6.41 us
  transfers between devices with their start and end apart: 4, of which 4 were waited for; matrix products, arithmetic and copies ran while one was open for 19% of the time, Pallas kernels for 0%

profile of v1, /device:TPU:0, one launch (start us, length us, event | category | flops | bytes accessed | tf_op | source)
XLA Modules:
  0.0 298.1 jit_solution(9268033333544835455)
XLA Ops:
  0.6 0.0 copy-start
  0.6 0.9 copy.27
  1.6 0.7 broadcast_multiply_fusion
  2.3 1.2 fusion.32
  3.5 1.2 fusion.25
  4.8 1.6 broadcast_in_dim.11
  6.4 2.2 reshape.137
  8.6 0.1 eq.15
  8.7 0.2 convert_reduce_fusion
  8.9 0.1 copy.26
  9.0 0.1 mul.121
  9.2 4.4 %scatter_custom_fusion = bf16[512,2048]{1,0:T(8,128)(2,1)} fusion(s32[256]{0:T(256)S(1)} %bitcast.53, bf16[256,2048]{1,0:T(8,128)(2,1)} %reshape.137, bf16[]{:T(256)} %constant.8.clone.1), kind=kCustom, calls=%fused_computation.51 | custom fusion | bytes 2097664 | tf_op jit(solution)/shard_map/scatter | solution.py:79
  13.6 0.0 copy-start.2
  13.6 7.4 %all-to-all-start = ((bf16[32,16,2048]{2,1,0:T(8,128)(2,1)}), bf16[32,16,2048]{2,1,0:T(8,128)(2,1)}, u32[]{:S(2)}, u32[]{:S(2)}) async-start(bf16[32,16,2048]{2,1,0:T(8,128)(2,1)} %bitcast.50), calls=%async_computation | async-start | bytes 4194304 | tf_op jit(solution)/shard_map/all_to_all | solution.py:10
  21.0 0.0 copy-done.2
  21.0 0.1 copy.25
  21.2 0.1 mul.132
  21.3 3.4 %mul.130 = f32[128,2,2048]{2,1,0:T(2,128)} broadcast(bf16[128,2048]{1,0:T(8,128)(2,1)} %param.15), dimensions={0,2} | broadcast | bytes 2621440 | tf_op jit(solution)/shard_map/mul | solution.py:99
  24.7 3.6 %mul.134 = f32[256,2048]{1,0:T(8,128)} reshape(f32[128,2,2048]{2,1,0:T(2,128)} %mul.130) | data formatting | bytes 4194304 | tf_op jit(solution)/shard_map/mul | solution.py:99
  28.4 4.8 %scatter_custom_fusion.1 = bf16[512,2048]{1,0:T(8,128)(2,1)} fusion(s32[256]{0:T(256)S(1)} %bitcast.54, f32[256,2048]{1,0:T(8,128)} %mul.134, f32[256]{0:T(256)S(1)} %mul.132, bf16[]{:T(256)} %constant.8.clone.1), kind=kCustom, calls=%fused_computation.48 | custom fusion | flops 1048576 | bytes 4195330 | tf_op jit(solution)/shard_map/scatter | solution.py:85
  33.2 35.3 %all-to-all-done = bf16[32,16,2048]{2,1,0:T(8,128)(2,1)} async-done(((bf16[32,16,2048]{2,1,0:T(8,128)(2,1)}), bf16[32,16,2048]{2,1,0:T(8,128)(2,1)}, u32[]{:S(2)}, u32[]{:S(2)}) %all-to-all-start) | async-done | bytes 2097184 | tf_op jit(solution)/shard_map/all_to_all | solution.py:10
  68.5 4.5 %all-to-all-start.2 = ((bf16[32,16,2048]{2,1,0:T(8,128)(2,1)}), bf16[32,16,2048]{2,1,0:T(8,128)(2,1)}, u32[]{:S(2)}, u32[]{:S(2)}) async-start(bf16[32,16,2048]{2,1,0:T(8,128)(2,1)} %bitcast.49), calls=%async_computation.2 | async-start | bytes 4194304 | tf_op jit(solution)/shard_map/all_to_all | solution.py:10
  73.0 5.5 %fusion.6 = f32[512,768]{1,0:T(8,128)} fusion(bf16[512,2048]{1,0:T(8,128)(2,1)} %bitcast.3, bf16[1,2048,768]{2,1,0:T(8,128)(2,1)} %param.13), kind=kOutput, calls=%fused_computation.14 | convolution fusion | flops 1610612736 | bytes 6815744 | tf_op jit(solution)/shard_map/dot_general | solution.py:29
  78.4 41.4 %all-to-all-done.2 = bf16[32,16,2048]{2,1,0:T(8,128)(2,1)} async-done(((bf16[32,16,2048]{2,1,0:T(8,128)(2,1)}), bf16[32,16,2048]{2,1,0:T(8,128)(2,1)}, u32[]{:S(2)}, u32[]{:S(2)}) %all-to-all-start.2) | async-done | bytes 2097184 | tf_op jit(solution)/shard_map/all_to_all | solution.py:10
  119.8 0.0 copy-start.8
  119.9 4.5 %fusion = f32[512,768]{1,0:T(8,128)S(1)} fusion(bf16[512,2048]{1,0:T(8,128)(2,1)} %bitcast.10, bf16[1,768,2048]{2,1,0:T(8,128)(2,1)} %param.14), kind=kOutput, calls=%fused_computation.8 | convolution fusion | flops 1610612736 | bytes 6815744 | tf_op jit(solution)/shard_map/dot_general | solution.py:22
  124.3 0.0 copy-done
  124.3 0.0 copy-done.8
  124.3 0.0 copy-start.3
  124.4 5.0 %multiply_convert_fusion.2 = (bf16[512,768]{1,0:T(8,128)(2,1)S(1)}, bf16[512,768]{1,0:T(8,128)(2,1)S(1)}, bf16[512,768]{1,0:T(8,128)(2,1)}) fusion(f32[512,768]{1,0:T(8,128)S(1)} %fusion, f32[512,768]{1,0:T(8,128)S(1)} %copy-done.8, bf16[512,2048]{1,0:T(8,128)(2,1)} %bitcast.3, bf16[1,2048,768]{2,1,0:T(8,128)(2,1)S(1)} %copy-done), kind=kOutput, calls=%fused_computation.28 | convolution fusion | flops 1616510976 | bytes 10747904 | tf_op jit(solution)/shard_map/dot_general | solution.py:28
  129.3 0.0 copy-start.5
  129.3 0.0 copy-start.4
  129.3 0.0 copy-done.3
  129.3 1.8 fusion.4
  131.2 0.0 copy-done.5
  131.2 0.0 copy-done.4
  131.2 3.2 %add_convert_fusion = bf16[512,2048]{1,0:T(8,128)(2,1)} fusion(f32[512,2048]{1,0:T(8,128)S(1)} %fusion.4, bf16[512,768]{1,0:T(8,128)(2,1)S(1)} %get-tuple-element.25, bf16[1,2048,768]{2,1,0:T(8,128)(2,1)S(1)} %copy-done), kind=kOutput, calls=%fused_computation.4 | convolution fusion | flops 1612709888 | bytes 10223616 | tf_op jit(solution)/shard_map/dot_general | solution.py:22
  134.3 4.7 %all-to-all-start.3 = ((bf16[32,16,2048]{2,1,0:T(8,128)(2,1)}), bf16[32,16,2048]{2,1,0:T(8,128)(2,1)}, u32[]{:S(2)}, u32[]{:S(2)}) async-start(bf16[32,16,2048]{2,1,0:T(8,128)(2,1)} %bitcast.52), calls=%async_computation.3 | async-start | bytes 4194304 | tf_op jit(solution)/shard_map/all_to_all | solution.py:17
  139.1 5.2 %fusion.12 = bf16[512,2048]{1,0:T(8,128)(2,1)} fusion(bf16[512,768]{1,0:T(8,128)(2,1)} %get-tuple-element.27, bf16[1,768,2048]{2,1,0:T(8,128)(2,1)} %param.14), kind=kOutput, calls=%fused_computation.20 | convolution fusion | flops 1611661312 | bytes 6029312 | tf_op jit(solution)/shard_map/dot_general | solution.py:33
  144.3 42.1 %all-to-all-done.3 = bf16[32,16,2048]{2,1,0:T(8,128)(2,1)} async-done(((bf16[32,16,2048]{2,1,0:T(8,128)(2,1)}), bf16[32,16,2048]{2,1,0:T(8,128)(2,1)}, u32[]{:S(2)}, u32[]{:S(2)}) %all-to-all-start.3) | async-done | bytes 2097184 | tf_op jit(solution)/shard_map/all_to_all | solution.py:17
  186.4 4.7 %all-to-all-start.1 = ((bf16[32,16,2048]{2,1,0:T(8,128)(2,1)}), bf16[32,16,2048]{2,1,0:T(8,128)(2,1)}, u32[]{:S(2)}, u32[]{:S(2)}) async-start(bf16[32,16,2048]{2,1,0:T(8,128)(2,1)} %bitcast.51), calls=%async_computation.1 | async-start | bytes 4194304 | tf_op jit(solution)/shard_map/all_to_all | solution.py:17
  191.1 2.1 convert_element_type.70
  193.2 0.0 copy-start.6
  193.2 5.3 %fusion.15 = bf16[1,2048,768]{2,1,0:T(8,128)(2,1)} fusion(bf16[512,2048]{1,0:T(8,128)(2,1)} %bitcast.3, bf16[512,768]{1,0:T(8,128)(2,1)} %copy-done.4), kind=kOutput, calls=%fused_computation.21 | convolution fusion | flops 1612185600 | bytes 6029312 | tf_op jit(solution)/shard_map/dot_general | solution.py:22
  198.5 0.0 copy-done.6
  198.5 0.0 copy-start.7
  198.5 5.2 %fusion.16 = bf16[1,2048,768]{2,1,0:T(8,128)(2,1)} fusion(bf16[512,2048]{1,0:T(8,128)(2,1)} %bitcast.3, bf16[512,768]{1,0:T(8,128)(2,1)S(1)} %copy-done.6), kind=kOutput, calls=%fused_computation.22 | convolution fusion | flops 1612185600 | bytes 6029312 | tf_op jit(solution)/shard_map/dot_general | solution.py:22
  203.7 0.0 copy-done.7
  203.7 5.1 %fusion.17 = bf16[1,768,2048]{2,1,0:T(8,128)(2,1)} fusion(bf16[512,768]{1,0:T(8,128)(2,1)S(1)} %copy-done.7, bf16[512,2048]{1,0:T(8,128)(2,1)} %bitcast.10), kind=kOutput, calls=%fused_computation.23 | convolution fusion | flops 1612185600 | bytes 6029312 | tf_op jit(solution)/shard_map/dot_general | solution.py:22
  208.8 5.2 %gather_fusion.1 = bf16[256,2048]{1,0:T(8,128)(2,1)} fusion(bf16[512,2048]{1,0:T(8,128)(2,1)} %bitcast.12, s32[1024]{0:T(1024)S(1)} %pad_clamp_fusion), kind=kCustom, calls=%fused_computation.1 | custom fusion | bytes 2098176 | tf_op jit(solution)/shard_map/gather | solution.py:96
  214.0 3.4 %reshape.116 = f32[128,2,2048]{2,1,0:T(2,128)} reshape(bf16[256,2048]{1,0:T(8,128)(2,1)} %gather_fusion.1) | data formatting | bytes 3145728 | tf_op jit(solution)/shard_map/convert_element_type | solution.py:96
  217.4 0.0 copy-start.1
  217.4 5.1 %reduce_sum.70 = f32[128,2048]{1,0:T(8,128)} reduce(f32[128,2,2048]{2,1,0:T(2,128)} %reshape.116, f32[]{:T(128)} %constant.5.clone.1), dimensions={1}, to_apply=%region_6.0 | reduce | flops 262144 | bytes 3145732 | tf_op jit(solution)/shard_map/reduce_sum | solution.py:95
  222.6 0.0 copy-done.1
  222.6 1.8 fusion.27
  224.3 13.5 %all-to-all-done.1 = bf16[32,16,2048]{2,1,0:T(8,128)(2,1)} async-done(((bf16[32,16,2048]{2,1,0:T(8,128)(2,1)}), bf16[32,16,2048]{2,1,0:T(8,128)(2,1)}, u32[]{:S(2)}, u32[]{:S(2)}) %all-to-all-start.1) | async-done | bytes 2097184 | tf_op jit(solution)/shard_map/all_to_all | solution.py:17
  237.8 5.2 %gather_fusion = bf16[256,2048]{1,0:T(8,128)(2,1)} fusion(bf16[512,2048]{1,0:T(8,128)(2,1)} %bitcast.8, s32[1024]{0:T(1024)S(1)} %pad_clamp_fusion), kind=kCustom, calls=%fused_computation | custom fusion | bytes 2098176 | tf_op jit(solution)/shard_map/gather | solution.py:84
  243.0 3.4 %reshape.115 = f32[128,2,2048]{2,1,0:T(2,128)} reshape(bf16[256,2048]{1,0:T(8,128)(2,1)} %gather_fusion) | data formatting | bytes 3145728 | tf_op jit(solution)/shard_map/convert_element_type | solution.py:84
  246.4 41.3 %psum.7 = f32[2048]{0:T(1024)} all-reduce(f32[2048]{0:T(1024)S(1)} %get-tuple-element.24), channel_id=1, replica_groups=mesh['expert'=8,'dp'=4] {'expert','dp'}, use_global_device_ids=true, to_apply=%region_8.0 | all-reduce | flops 2048 | bytes 16384 | tf_op jit(solution)/shard_map/psum | solution.py:101
  287.7 6.4 %multiply_reduce_fusion = (f32[128,2]{1,0:T(8,128)S(1)}, f32[128,2048]{1,0:T(8,128)}) fusion(f32[128,2,2048]{2,1,0:T(2,128)} %reshape.115, f32[128,2048]{1,0:T(8,128)} %convert_element_type.70, f32[128,2]{1,0:T(8,128)S(1)} %copy.25), kind=kLoop, calls=%fused_computation.25 | loop fusion | flops 1834752 | bytes 4196352 | tf_op jit(solution)/shard_map/reduce_sum | solution.py:99
  294.2 0.6 copy.29
  294.8 3.3 %fusion.31 = (bf16[128,2048]{1,0:T(8,128)(2,1)}, bf16[128,2048]{1,0:T(8,128)(2,1)}) fusion(bf16[128,2048]{1,0:T(8,128)(2,1)} %param.8, f32[128,2048]{1,0:T(8,128)} %reduce_sum.70, f32[128]{0:T(128)S(1)} %broadcast_multiply_fusion.1, f32[2048]{0:T(1024)S(1)} %copy-done.1, f32[128]{0:T(128)S(1)} %add_rsqrt_fusion, bf16[128,2048]{1,0:T(8,128)(2,1)} %param.15, ...), kind=kLoop, calls=%fused_computation.45 | loop fusion | flops 2883584 | bytes 4203520 | tf_op jit(solution)/shard_map/convert_element_type | solution.py:107
  (4 shorter events, 0.0 us)
Async XLA Ops:
  0.6 123.7 %copy-start = (bf16[1,2048,768]{2,1,0:T(8,128)(2,1)S(1)}, bf16[1,2048,768]{2,1,0:T(8,128)(2,1)}, u32[]{:S(2)}) copy-start(bf16[1,2048,768]{2,1,0:T(8,128)(2,1)} %param.12) | copy-start | bytes 9437188
  13.6 7.4 %copy-start.2 = (f32[128,2]{0,1:T(2,128)S(1)}, f32[128,2]{0,1:T(2,128)}, u32[]{:S(2)}) copy-start(f32[128,2]{0,1:T(2,128)} %param.10) | copy-start | bytes 3076
  13.6 54.9 %all-to-all-start = ((bf16[32,16,2048]{2,1,0:T(8,128)(2,1)}), bf16[32,16,2048]{2,1,0:T(8,128)(2,1)}, u32[]{:S(2)}, u32[]{:S(2)}) async-start(bf16[32,16,2048]{2,1,0:T(8,128)(2,1)} %bitcast.50), calls=%async_computation | async-start | bytes 4194304 | tf_op jit(solution)/shard_map/all_to_all | solution.py:10
  68.5 51.3 %all-to-all-start.2 = ((bf16[32,16,2048]{2,1,0:T(8,128)(2,1)}), bf16[32,16,2048]{2,1,0:T(8,128)(2,1)}, u32[]{:S(2)}, u32[]{:S(2)}) async-start(bf16[32,16,2048]{2,1,0:T(8,128)(2,1)} %bitcast.49), calls=%async_computation.2 | async-start | bytes 4194304 | tf_op jit(solution)/shard_map/all_to_all | solution.py:10
  119.8 4.5 %copy-start.8 = (f32[512,768]{1,0:T(8,128)S(1)}, f32[512,768]{1,0:T(8,128)}, u32[]{:S(2)}) copy-start(f32[512,768]{1,0:T(8,128)} %fusion.6) | copy-start | bytes 4718596
  124.3 5.0 %copy-start.3 = (bf16[1,2048,768]{2,1,0:T(8,128)(2,1)S(1)}, bf16[1,2048,768]{2,1,0:T(8,128)(2,1)}, u32[]{:S(2)}) copy-start(bf16[1,2048,768]{2,1,0:T(8,128)(2,1)} %param.13) | copy-start | bytes 9437188
  129.3 1.8 copy-start.5
  129.3 1.8 copy-start.4
  134.3 52.0 %all-to-all-start.3 = ((bf16[32,16,2048]{2,1,0:T(8,128)(2,1)}), bf16[32,16,2048]{2,1,0:T(8,128)(2,1)}, u32[]{:S(2)}, u32[]{:S(2)}) async-start(bf16[32,16,2048]{2,1,0:T(8,128)(2,1)} %bitcast.52), calls=%async_computation.3 | async-start | bytes 4194304 | tf_op jit(solution)/shard_map/all_to_all | solution.py:17
  186.4 51.5 %all-to-all-start.1 = ((bf16[32,16,2048]{2,1,0:T(8,128)(2,1)}), bf16[32,16,2048]{2,1,0:T(8,128)(2,1)}, u32[]{:S(2)}, u32[]{:S(2)}) async-start(bf16[32,16,2048]{2,1,0:T(8,128)(2,1)} %bitcast.51), calls=%async_computation.1 | async-start | bytes 4194304 | tf_op jit(solution)/shard_map/all_to_all | solution.py:17
  193.2 5.3 %copy-start.6 = (bf16[512,768]{1,0:T(8,128)(2,1)S(1)}, bf16[512,768]{1,0:T(8,128)(2,1)}, u32[]{:S(2)}) copy-start(bf16[512,768]{1,0:T(8,128)(2,1)} %copy-done.5) | copy-start | bytes 2359300
  198.5 5.2 %copy-start.7 = (bf16[512,768]{1,0:T(8,128)(2,1)S(1)}, bf16[512,768]{1,0:T(8,128)(2,1)}, u32[]{:S(2)}) copy-start(bf16[512,768]{1,0:T(8,128)(2,1)} %get-tuple-element.27) | copy-start | bytes 2359300
  217.4 5.1 %copy-start.1 = (f32[2048]{0:T(1024)S(1)}, f32[2048]{0:T(1024)}, u32[]{:S(2)}) copy-start(f32[2048]{0:T(1024)} %param.11) | copy-start | bytes 24580

commit v2 on v1

v2 whole, which is shorter than its diff:
```python
import jax
import jax.numpy as jnp
from jax import lax
from jax.sharding import PartitionSpec as P

BOTH = ("expert", "dp")


def contract(left, right, left_dim, right_dim):
    return lax.dot_general(
        left, right, (((left_dim,), (right_dim,)), ((), ())), preferred_element_type=jnp.float32
    )


def exchange(rows):
    shaped = rows.reshape(lax.axis_size(BOTH), -1, rows.shape[-1])
    return lax.all_to_all(shaped, BOTH, split_axis=0, concat_axis=0, tiled=True).reshape(
        rows.shape
    )


def slots_of(routes, capacity):
    columns = [routes[:, k] for k in range(routes.shape[1])]
    places = jnp.arange(routes.shape[0], dtype=jnp.int32)
    earlier = places[None, :] < places[:, None]
    return [
        own * capacity
        + jnp.sum(
            sum(((own[:, None] == other[None, :]) & earlier).astype(jnp.int32) for other in columns),
            axis=1,
        )
        for own in columns
    ]


def on_device(tokens, routes, gate_probs, norm_gain, w_gate, w_up, w_down, out_grad):
    devices_all = lax.axis_size(BOTH)
    tok_rows, width = tokens.shape
    top_count = routes.shape[1]
    capacity = 2 * tok_rows * top_count // devices_all
    gate_matrix, up_matrix, down_matrix = w_gate[0], w_up[0], w_down[0]

    inputs = tokens.astype(jnp.float32)
    inverse_rms = lax.rsqrt(jnp.mean(inputs * inputs, axis=1, keepdims=True) + 1e-06)
    normed = inputs * inverse_rms
    scaled = (normed * norm_gain).astype(jnp.bfloat16)

    numbers = jnp.arange(devices_all * capacity, dtype=jnp.int32)[:, None]
    hits = [slot[None, :] == numbers for slot in slots_of(routes, capacity)]
    picks = [h.astype(jnp.bfloat16) for h in hits]
    chosen = sum(picks)
    slot_weight = sum(
        jnp.sum(jnp.where(h, gate_probs[None, :, k], 0.0), axis=1) for k, h in enumerate(hits)
    )[:, None]

    arrived = exchange(contract(chosen, scaled, 1, 0).astype(jnp.bfloat16))
    arrived_grad = exchange(
        (slot_weight * contract(chosen, out_grad, 1, 0)).astype(jnp.bfloat16)
    )

    pre_gate = contract(arrived, gate_matrix, 1, 0)
    up_value = contract(arrived, up_matrix, 1, 0)
    sigmoid_gate = jax.nn.sigmoid(pre_gate)
    activated = pre_gate * sigmoid_gate
    hidden = (activated * up_value).astype(jnp.bfloat16)
    expert_out = contract(hidden, down_matrix, 1, 0).astype(jnp.bfloat16)
    expert_out, arrived_grad = lax.optimization_barrier((expert_out, arrived_grad))
    returned = exchange(expert_out)

    grad_hidden = contract(arrived_grad, down_matrix, 1, 1)
    grad_pre = (
        grad_hidden * up_value * sigmoid_gate * (1.0 + pre_gate * (1.0 - sigmoid_gate))
    ).astype(jnp.bfloat16)
    grad_upval = (grad_hidden * activated).astype(jnp.bfloat16)
    grad_back = (
        contract(grad_pre, gate_matrix, 1, 1) + contract(grad_upval, up_matrix, 1, 1)
    ).astype(jnp.bfloat16)
    returned, grad_back = lax.optimization_barrier((returned, grad_back))
    returned_grad = exchange(grad_back)
    grad_down = contract(hidden, arrived_grad, 0, 0).astype(jnp.bfloat16)
    grad_gate = contract(arrived, grad_pre, 0, 0).astype(jnp.bfloat16)
    grad_up = contract(arrived, grad_upval, 0, 0).astype(jnp.bfloat16)

    grad_in = out_grad.astype(jnp.float32)
    picked = [contract(pick, returned, 0, 0) for pick in picks]
    mixed = (inputs + sum(gate_probs[:, k : k + 1] * p for k, p in enumerate(picked))).astype(
        jnp.bfloat16
    )
    grad_probs = jnp.stack([jnp.sum(grad_in * p, axis=1) for p in picked], axis=1)

    grad_normed = contract(chosen, returned_grad, 0, 0)
    gain_part = jnp.sum(grad_normed * normed, axis=0)
    parts = exchange(jnp.broadcast_to(gain_part[None, :], (devices_all, width)))
    grad_gain = jnp.sum(parts, axis=0)
    grad_scaled = grad_normed * norm_gain
    grad_tokens = (
        grad_in
        + inverse_rms
        * (grad_scaled - normed * jnp.mean(grad_scaled * normed, axis=1, keepdims=True))
    ).astype(jnp.bfloat16)
    return (
        mixed,
        grad_probs,
        grad_gain,
        grad_tokens,
        grad_gate[None],
        grad_up[None],
        grad_down[None],
    )


def solution(mesh):
    rows, copied, blocks = P(BOTH, None), P(), P(BOTH, None, None)
    return jax.shard_map(
        on_device,
        mesh=mesh,
        in_specs=(rows, rows, rows, copied, blocks, blocks, blocks, rows),
        out_specs=(rows, rows, copied, rows, blocks, blocks, blocks),
        check_vma=False,
    )
```

time: 299 us -> 237 us (0.79)
  blocking collectives: 41.3 us -> 0 us
  local copies, waits for them, and re-layouts: 34.8 us -> 3.12 us
  other arithmetic: 26.9 us -> 3.9 us
  waiting for transfers between devices: 132 us -> 148 us
  matrix products: 40.7 us -> 55.2 us
  starting transfers between devices: 21.3 us -> 25.4 us
    psum x1 -> x0, blocking collectives: 41.3 us -> none  [on_device(): grad_gain = lax.psum(gain_part, ('expert', 'dp'))]
    dot_general x6 -> x14, matrix products: 25 us -> 55.2 us  [contract(): lax.dot_general(left, right, (((left_dim,), (right_dim,)), ((), ())), pre...]
    dot_general x3 -> x0, matrix products: 15.7 us -> none  [the longest x1 5.45 us: forward_expert(): up_value = jnp.dot(arrived, up_matrix, preferred_element_type=jnp.float32)]
    all_to_all x4 -> x5, waiting for transfers between devices: 132 us -> 148 us  [exchange(): lax.all_to_all(shaped, BOTH, split_axis=0, concat_axis=0, tiled=True)]
    reduce_sum x4 -> x3, other arithmetic: 13.5 us -> 1.16 us  [the longest x1 0.76 us: on_device(): grad_gain = jnp.sum(parts, axis=0)]
    gather x2 -> x0, local copies, waits for them, and re-layouts: 10.4 us -> none  [the longest x1 5.23 us: on_device(): returned_grad[slot_index].reshape(tok_rows, top_count, width)]
    mul x5 -> x0, local copies, waits for them, and re-layouts: 7.46 us -> none  [the longest x2 7.06 us: on_device(): grad_probs = jnp.sum(grad_in[:, None, :] * picked, axis=2)]
    convert_element_type x2 -> x0, local copies, waits for them, and re-layouts: 6.77 us -> none  [the longest x1 3.39 us: on_device(): returned[slot_index].reshape(tok_rows, top_count, width).astype(jnp.float32)]
  transfers between devices with their start and end apart: 4 -> 5, of which waited for: 4 -> 5; matrix products, arithmetic and copies ran while one was open for 19% -> 21% of each run, Pallas kernels for 0% -> 0%
where the time goes in v2:
time: 237 us; the launch traced here: 236 us
  waiting for transfers between devices  148 us (62%)
  matrix products  55.2 us (23%)
  starting transfers between devices  25.4 us (11%)
  other arithmetic  3.9 us (2%)
  local copies, waits for them, and re-layouts  3.12 us (1%)
    all_to_all x5, waiting for transfers between devices, exchange(): lax.all_to_all(shaped, BOTH, split_axis=0, concat_axis=0, tiled=True)  148 us
    dot_general x14, matrix products, contract(): lax.dot_general(left, right, (((left_dim,), (right_dim,)), ((), ())), pre...  55.2 us
    all_to_all x5, starting transfers between devices, exchange(): lax.all_to_all(shaped, BOTH, split_axis=0, concat_axis=0, tiled=True)  25.4 us
  transfers between devices with their start and end apart: 5, of which 5 were waited for; matrix products, arithmetic and copies ran while one was open for 21% of the time, Pallas kernels for 0%

profile of v2, /device:TPU:0, one launch (start us, length us, event | category | flops | bytes accessed | tf_op | source)
XLA Modules:
  0.0 236.3 jit_solution(11311373123424372948)
XLA Ops:
  0.6 0.0 copy-start
  0.6 1.4 fusion.30
  2.0 0.8 slice_bitcast_fusion.2
  2.8 0.2 add_reduce_fusion.1
  3.0 0.8 multiply_add_fusion.1
  3.7 3.2 %convolution_convert_fusion.3 = bf16[512,2048]{1,0:T(8,128)(2,1)} fusion(bf16[128,2048]{1,0:T(8,128)(2,1)} %param.8, f32[2048]{0:T(1024)} %param.11, f32[128]{0:T(128)S(1)} %add_rsqrt_fusion, s32[128]{0:T(128)S(1)} %get-tuple-element.28, s32[128]{0:T(128)S(1)} %get-tuple-element.27), kind=kOutput, calls=%fused_computation.17 | convolution fusion | flops 271056896 | bytes 2631168 | tf_op jit(solution)/shard_map/dot_general | solution.py:10
  6.9 0.0 copy-start.2
  6.9 7.4 %all-to-all-start = ((bf16[32,16,2048]{2,1,0:T(8,128)(2,1)}), bf16[32,16,2048]{2,1,0:T(8,128)(2,1)}, u32[]{:S(2)}, u32[]{:S(2)}) async-start(bf16[32,16,2048]{2,1,0:T(8,128)(2,1)} %bitcast.67), calls=%async_computation | async-start | bytes 4194304 | tf_op jit(solution)/shard_map/all_to_all | solution.py:17
  14.3 0.0 copy-done.2
  14.4 0.2 select_reduce_fusion
  14.6 3.1 %multiply_convert_fusion = bf16[512,2048]{1,0:T(8,128)(2,1)} fusion(bf16[128,2048]{1,0:T(8,128)(2,1)} %param.15, f32[512]{0:T(512)S(1)} %add.67, s32[128]{0:T(128)S(1)} %get-tuple-element.28, s32[128]{0:T(128)S(1)} %get-tuple-element.27), kind=kOutput, calls=%fused_computation.1 | convolution fusion | flops 271056896 | bytes 2624512 | tf_op jit(solution)/shard_map/dot_general | solution.py:10
  17.7 44.2 %all-to-all-done = bf16[32,16,2048]{2,1,0:T(8,128)(2,1)} async-done(((bf16[32,16,2048]{2,1,0:T(8,128)(2,1)}), bf16[32,16,2048]{2,1,0:T(8,128)(2,1)}, u32[]{:S(2)}, u32[]{:S(2)}) %all-to-all-start) | async-done | bytes 2097184 | tf_op jit(solution)/shard_map/all_to_all | solution.py:17
  61.8 4.3 %all-to-all-start.1 = ((bf16[32,16,2048]{2,1,0:T(8,128)(2,1)}), bf16[32,16,2048]{2,1,0:T(8,128)(2,1)}, u32[]{:S(2)}, u32[]{:S(2)}) async-start(bf16[32,16,2048]{2,1,0:T(8,128)(2,1)} %bitcast.68), calls=%async_computation.1 | async-start | bytes 4194304 | tf_op jit(solution)/shard_map/all_to_all | solution.py:17
  66.1 0.0 copy-start.3
  66.1 4.5 %fusion.10 = f32[512,768]{1,0:T(8,128)S(1)} fusion(bf16[512,2048]{1,0:T(8,128)(2,1)} %bitcast.4, bf16[1,2048,768]{2,1,0:T(8,128)(2,1)} %param.12), kind=kOutput, calls=%fused_computation.15 | convolution fusion | flops 1610612736 | bytes 6815744 | tf_op jit(solution)/shard_map/dot_general | solution.py:10
  70.6 0.0 copy-done.3
  70.6 0.0 copy-start.11
  70.6 5.2 %multiply_convert_fusion.3 = (bf16[512,768]{1,0:T(8,128)(2,1)S(1)}, f32[512,768]{1,0:T(8,128)}) fusion(f32[512,768]{1,0:T(8,128)S(1)} %fusion.10, bf16[512,2048]{1,0:T(8,128)(2,1)} %bitcast.4, bf16[1,2048,768]{2,1,0:T(8,128)(2,1)S(1)} %copy-done.3), kind=kOutput, calls=%fused_computation.27 | convolution fusion | flops 1612972032 | bytes 9175040 | tf_op jit(solution)/shard_map/dot_general | solution.py:10
  75.8 0.0 copy-done.11
  75.8 0.0 copy-start.9
  75.8 0.9 copy-done.9
  76.7 0.0 copy-done
  76.7 3.2 %fusion.12 = bf16[512,2048]{1,0:T(8,128)(2,1)} fusion(bf16[512,768]{1,0:T(8,128)(2,1)S(1)} %get-tuple-element.31, bf16[1,768,2048]{2,1,0:T(8,128)(2,1)S(1)} %copy-done), kind=kOutput, calls=%fused_computation.18 | convolution fusion | flops 1611661312 | bytes 6029312 | tf_op jit(solution)/shard_map/dot_general | solution.py:10
  79.8 33.6 %all-to-all-done.1 = bf16[32,16,2048]{2,1,0:T(8,128)(2,1)} async-done(((bf16[32,16,2048]{2,1,0:T(8,128)(2,1)}), bf16[32,16,2048]{2,1,0:T(8,128)(2,1)}, u32[]{:S(2)}, u32[]{:S(2)}) %all-to-all-start.1) | async-done | bytes 2097184 | tf_op jit(solution)/shard_map/all_to_all | solution.py:17
  113.4 4.4 %all-to-all-start.2 = ((bf16[32,16,2048]{2,1,0:T(8,128)(2,1)}), bf16[32,16,2048]{2,1,0:T(8,128)(2,1)}, u32[]{:S(2)}, u32[]{:S(2)}) async-start(bf16[32,16,2048]{2,1,0:T(8,128)(2,1)} %bitcast.69), calls=%async_computation.2 | async-start | bytes 4194304 | tf_op jit(solution)/shard_map/all_to_all | solution.py:17
  117.9 0.0 copy-start.4
  117.9 4.9 %multiply_convert_fusion.2 = (bf16[512,768]{1,0:T(8,128)(2,1)S(1)}, bf16[512,768]{1,0:T(8,128)(2,1)S(1)}) fusion(f32[512,768]{1,0:T(8,128)} %copy-done.11, f32[512,768]{1,0:T(8,128)} %get-tuple-element.32, bf16[512,2048]{1,0:T(8,128)(2,1)} %bitcast.10, bf16[1,768,2048]{2,1,0:T(8,128)(2,1)S(1)} %copy-done), kind=kOutput, calls=%fused_computation.26 | convolution fusion | flops 1615724544 | bytes 9961472 | tf_op jit(solution)/shard_map/dot_general | solution.py:10
  122.8 0.0 copy-start.7
  122.8 0.0 copy-start.6
  122.8 0.0 copy-done.4
  122.8 0.0 copy-start.5
  122.8 1.8 fusion.4
  124.7 0.0 copy-done.7
  124.7 0.0 copy-done.6
  124.7 0.6 copy-done.5
  125.3 3.2 %add_convert_fusion = bf16[512,2048]{1,0:T(8,128)(2,1)} fusion(f32[512,2048]{1,0:T(8,128)S(1)} %fusion.4, bf16[512,768]{1,0:T(8,128)(2,1)S(1)} %get-tuple-element.21, bf16[1,2048,768]{2,1,0:T(8,128)(2,1)S(1)} %copy-done.5), kind=kOutput, calls=%fused_computation | convolution fusion | flops 1612709888 | bytes 10223616 | tf_op jit(solution)/shard_map/dot_general | solution.py:10
  128.5 36.8 %all-to-all-done.2 = bf16[32,16,2048]{2,1,0:T(8,128)(2,1)} async-done(((bf16[32,16,2048]{2,1,0:T(8,128)(2,1)}), bf16[32,16,2048]{2,1,0:T(8,128)(2,1)}, u32[]{:S(2)}, u32[]{:S(2)}) %all-to-all-start.2) | async-done | bytes 2097184 | tf_op jit(solution)/shard_map/all_to_all | solution.py:17
  165.2 4.6 %all-to-all-start.3 = ((bf16[32,16,2048]{2,1,0:T(8,128)(2,1)}), bf16[32,16,2048]{2,1,0:T(8,128)(2,1)}, u32[]{:S(2)}, u32[]{:S(2)}) async-start(bf16[32,16,2048]{2,1,0:T(8,128)(2,1)} %bitcast.70), calls=%async_computation.3 | async-start | bytes 4194304 | tf_op jit(solution)/shard_map/all_to_all | solution.py:17
  169.9 0.0 copy-start.8
  169.9 5.3 %fusion.15 = bf16[1,2048,768]{2,1,0:T(8,128)(2,1)} fusion(bf16[512,2048]{1,0:T(8,128)(2,1)} %bitcast.4, bf16[512,768]{1,0:T(8,128)(2,1)} %copy-done.6), kind=kOutput, calls=%fused_computation.19 | convolution fusion | flops 1612185600 | bytes 6029312 | tf_op jit(solution)/shard_map/dot_general | solution.py:10
  175.2 0.0 copy-done.8
  175.2 0.0 copy-start.10
  175.2 5.2 %fusion.16 = bf16[1,2048,768]{2,1,0:T(8,128)(2,1)} fusion(bf16[512,2048]{1,0:T(8,128)(2,1)} %bitcast.4, bf16[512,768]{1,0:T(8,128)(2,1)S(1)} %copy-done.8), kind=kOutput, calls=%fused_computation.20 | convolution fusion | flops 1612185600 | bytes 6029312 | tf_op jit(solution)/shard_map/dot_general | solution.py:10
  180.4 0.0 copy-done.10
  180.4 5.1 %fusion.17 = bf16[1,768,2048]{2,1,0:T(8,128)(2,1)} fusion(bf16[512,768]{1,0:T(8,128)(2,1)S(1)} %copy-done.10, bf16[512,2048]{1,0:T(8,128)(2,1)} %bitcast.10), kind=kOutput, calls=%fused_computation.21 | convolution fusion | flops 1612185600 | bytes 6029312 | tf_op jit(solution)/shard_map/dot_general | solution.py:10
  185.5 0.0 copy-start.1
  185.5 3.1 %fusion.38 = f32[128,2048]{1,0:T(8,128)} fusion(bf16[512,2048]{1,0:T(8,128)(2,1)} %bitcast.12, s32[128]{0:T(128)S(1)} %get-tuple-element.28), kind=kOutput, calls=%fused_computation.52 | convolution fusion | flops 268500992 | bytes 3146240 | tf_op jit(solution)/shard_map/dot_general | solution.py:10
  188.6 28.1 %all-to-all-done.3 = bf16[32,16,2048]{2,1,0:T(8,128)(2,1)} async-done(((bf16[32,16,2048]{2,1,0:T(8,128)(2,1)}), bf16[32,16,2048]{2,1,0:T(8,128)(2,1)}, u32[]{:S(2)}, u32[]{:S(2)}) %all-to-all-start.3) | async-done | bytes 2097184 | tf_op jit(solution)/shard_map/all_to_all | solution.py:17
  216.7 0.0 copy-done.1
  216.7 3.2 %fusion.27 = (f32[128]{0:T(128)S(1)}, f32[2048]{0:T(1024)S(1)}, f32[128,2048]{1,0:T(8,128)}) fusion(bf16[128,2048]{1,0:T(8,128)(2,1)} %param.8, f32[2048]{0:T(1024)S(1)} %copy-done.1, f32[128]{0:T(128)S(1)} %add_rsqrt_fusion, bf16[512,2048]{1,0:T(8,128)(2,1)} %bitcast.16, s32[128]{0:T(128)S(1)} %get-tuple-element.28, s32[128]{0:T(128)S(1)} %get-tuple-element.27), kind=kOutput, calls=%fused_computation.39 | convolution fusion | flops 270792576 | bytes 3688448 | tf_op jit(solution)/shard_map/dot_general | solution.py:10
  219.9 0.8 reshape.89
  220.7 4.6 %all-to-all-start.4 = ((f32[32,1,2048]{2,1,0:T(1,128)}), f32[32,1,2048]{2,1,0:T(1,128)S(1)}, u32[]{:S(2)}, u32[]{:S(2)}) async-start(f32[32,1,2048]{2,1,0:T(1,128)} %reshape.89), calls=%async_computation.4 | async-start | bytes 524288 | tf_op jit(solution)/shard_map/all_to_all | solution.py:17
  225.3 4.4 %fusion.32 = (f32[128]{0:T(128)S(1)}, f32[128]{0:T(128)S(1)}, bf16[128,2048]{1,0:T(8,128)(2,1)}, bf16[128,2048]{1,0:T(8,128)(2,1)}) fusion(bf16[128,2048]{1,0:T(8,128)(2,1)} %param.15, f32[128,2048]{1,0:T(8,128)} %fusion.38, f32[128]{0:T(128)S(1)} %get-tuple-element.25, f32[128]{0:T(128)S(1)} %get-tuple-element.26, bf16[128,2048]{1,0:T(8,128)(2,1)} %param.8, ...), kind=kOutput, calls=%fused_computation.44 | convolution fusion | flops 273219328 | bytes 6303232 | tf_op jit(solution)/shard_map/dot_general | solution.py:10
  229.7 0.6 pad_maximum_fusion
  230.3 5.2 %all-to-all-done.4 = f32[32,1,2048]{2,1,0:T(1,128)S(1)} async-done(((f32[32,1,2048]{2,1,0:T(1,128)}), f32[32,1,2048]{2,1,0:T(1,128)S(1)}, u32[]{:S(2)}, u32[]{:S(2)}) %all-to-all-start.4) | async-done | bytes 262176 | tf_op jit(solution)/shard_map/all_to_all | solution.py:17
  235.5 0.8 reduce_sum.98
  (4 shorter events, 0.0 us)
Async XLA Ops:
  0.6 76.0 %copy-start = (bf16[1,768,2048]{2,1,0:T(8,128)(2,1)S(1)}, bf16[1,768,2048]{2,1,0:T(8,128)(2,1)}, u32[]{:S(2)}) copy-start(bf16[1,768,2048]{2,1,0:T(8,128)(2,1)} %param.14) | copy-start | bytes 9437188
  6.9 7.4 %copy-start.2 = (f32[128,2]{0,1:T(2,128)S(1)}, f32[128,2]{0,1:T(2,128)}, u32[]{:S(2)}) copy-start(f32[128,2]{0,1:T(2,128)} %param.10) | copy-start | bytes 3076
  6.9 54.9 %all-to-all-start = ((bf16[32,16,2048]{2,1,0:T(8,128)(2,1)}), bf16[32,16,2048]{2,1,0:T(8,128)(2,1)}, u32[]{:S(2)}, u32[]{:S(2)}) async-start(bf16[32,16,2048]{2,1,0:T(8,128)(2,1)} %bitcast.67), calls=%async_computation | async-start | bytes 4194304 | tf_op jit(solution)/shard_map/all_to_all | solution.py:17
  61.8 51.6 %all-to-all-start.1 = ((bf16[32,16,2048]{2,1,0:T(8,128)(2,1)}), bf16[32,16,2048]{2,1,0:T(8,128)(2,1)}, u32[]{:S(2)}, u32[]{:S(2)}) async-start(bf16[32,16,2048]{2,1,0:T(8,128)(2,1)} %bitcast.68), calls=%async_computation.1 | async-start | bytes 4194304 | tf_op jit(solution)/shard_map/all_to_all | solution.py:17
  66.1 4.5 %copy-start.3 = (bf16[1,2048,768]{2,1,0:T(8,128)(2,1)S(1)}, bf16[1,2048,768]{2,1,0:T(8,128)(2,1)}, u32[]{:S(2)}) copy-start(bf16[1,2048,768]{2,1,0:T(8,128)(2,1)} %param.13) | copy-start | bytes 9437188
  70.6 5.2 %copy-start.11 = (f32[512,768]{1,0:T(8,128)}, f32[512,768]{1,0:T(8,128)S(1)}, u32[]{:S(2)}) copy-start(f32[512,768]{1,0:T(8,128)S(1)} %fusion.10) | copy-start | bytes 4718596
  75.8 0.9 copy-start.9
  113.4 51.8 %all-to-all-start.2 = ((bf16[32,16,2048]{2,1,0:T(8,128)(2,1)}), bf16[32,16,2048]{2,1,0:T(8,128)(2,1)}, u32[]{:S(2)}, u32[]{:S(2)}) async-start(bf16[32,16,2048]{2,1,0:T(8,128)(2,1)} %bitcast.69), calls=%async_computation.2 | async-start | bytes 4194304 | tf_op jit(solution)/shard_map/all_to_all | solution.py:17
  117.9 4.9 %copy-start.4 = (bf16[1,2048,768]{2,1,0:T(8,128)(2,1)S(1)}, bf16[1,2048,768]{2,1,0:T(8,128)(2,1)}, u32[]{:S(2)}) copy-start(bf16[1,2048,768]{2,1,0:T(8,128)(2,1)} %param.13) | copy-start | bytes 9437188
  122.8 1.9 copy-start.7
  122.8 1.9 copy-start.6
  122.8 2.4 %copy-start.5 = (bf16[1,2048,768]{2,1,0:T(8,128)(2,1)S(1)}, bf16[1,2048,768]{2,1,0:T(8,128)(2,1)}, u32[]{:S(2)}) copy-start(bf16[1,2048,768]{2,1,0:T(8,128)(2,1)} %param.12) | copy-start | bytes 9437188
  165.2 51.5 %all-to-all-start.3 = ((bf16[32,16,2048]{2,1,0:T(8,128)(2,1)}), bf16[32,16,2048]{2,1,0:T(8,128)(2,1)}, u32[]{:S(2)}, u32[]{:S(2)}) async-start(bf16[32,16,2048]{2,1,0:T(8,128)(2,1)} %bitcast.70), calls=%async_computation.3 | async-start | bytes 4194304 | tf_op jit(solution)/shard_map/all_to_all | solution.py:17
  169.9 5.3 %copy-start.8 = (bf16[512,768]{1,0:T(8,128)(2,1)S(1)}, bf16[512,768]{1,0:T(8,128)(2,1)}, u32[]{:S(2)}) copy-start(bf16[512,768]{1,0:T(8,128)(2,1)} %copy-done.7) | copy-start | bytes 2359300
  175.2 5.2 %copy-start.10 = (bf16[512,768]{1,0:T(8,128)(2,1)S(1)}, bf16[512,768]{1,0:T(8,128)(2,1)}, u32[]{:S(2)}) copy-start(bf16[512,768]{1,0:T(8,128)(2,1)} %copy-done.9) | copy-start | bytes 2359300
  185.5 31.2 %copy-start.1 = (f32[2048]{0:T(1024)S(1)}, f32[2048]{0:T(1024)}, u32[]{:S(2)}) copy-start(f32[2048]{0:T(1024)} %param.11) | copy-start | bytes 24580
  220.7 14.8 %all-to-all-start.4 = ((f32[32,1,2048]{2,1,0:T(1,128)}), f32[32,1,2048]{2,1,0:T(1,128)S(1)}, u32[]{:S(2)}, u32[]{:S(2)}) async-start(f32[32,1,2048]{2,1,0:T(1,128)} %reshape.89), calls=%async_computation.4 | async-start | bytes 524288 | tf_op jit(solution)/shard_map/all_to_all | solution.py:17

commit v3 on v2

--- a/solution.py
+++ b/solution.py
@@ -1,6 +1,8 @@
 import jax
 import jax.numpy as jnp
 from jax import lax
+from jax.experimental import pallas as pl
+from jax.experimental.pallas import tpu as pltpu
 from jax.sharding import PartitionSpec as P
 
 BOTH = ("expert", "dp")
@@ -31,6 +33,53 @@
         )
         for own in columns
     ]
+
+
+def total_over_devices(part):
+    for axis in reversed(BOTH):
+        size, apart = lax.axis_size(axis), 1
+        while apart < size:
+            part = part + lax.ppermute(part, axis, [(i, i ^ apart) for i in range(size)])
+            apart *= 2
+    return part
+
+
+def tokens_gradient_kernel(chosen_ref, back_ref, tokens_ref, gain_ref, grad_ref, out_ref):
+    inputs = tokens_ref[...].astype(jnp.float32)
+    inverse_rms = lax.rsqrt(jnp.mean(inputs * inputs, axis=1, keepdims=True) + 1e-06)
+    normed = inputs * inverse_rms
+    grad_normed = contract(chosen_ref[...], back_ref[...], 1, 0)
+    grad_scaled = grad_normed * gain_ref[...]
+    mean = jnp.mean(grad_scaled * normed, axis=1, keepdims=True)
+    out_ref[...] = (
+        grad_ref[...].astype(jnp.float32) + inverse_rms * (grad_scaled - normed * mean)
+    ).astype(jnp.bfloat16)
+
+
+def tokens_gradient(chosen, returned_grad, tokens, norm_gain, out_grad):
+    rows, width = tokens.shape
+    slots = chosen.shape[0]
+    step = min(64, rows)
+    own = pl.BlockSpec((step, width), lambda i: (i, 0))
+    return pl.pallas_call(
+        tokens_gradient_kernel,
+        grid=(rows // step,),
+        out_shape=jax.ShapeDtypeStruct((rows, width), jnp.bfloat16),
+        in_specs=[
+            pl.BlockSpec((step, slots), lambda i: (i, 0)),
+            pl.BlockSpec((slots, width), lambda i: (0, 0)),
+            own,
+            pl.BlockSpec((1, width), lambda i: (0, 0)),
+            own,
+        ],
+        out_specs=own,
+        compiler_params=pltpu.CompilerParams(vmem_limit_bytes=24 * 2**20),
+        cost_estimate=pl.CostEstimate(
+            flops=2 * rows * slots * width,
+            bytes_accessed=2 * width * (slots + 3 * rows),
+            transcendentals=0,
+        ),
+    )(chosen.T, returned_grad, tokens, norm_gain[None, :], out_grad)
 
 
 def on_device(tokens, routes, gate_probs, norm_gain, w_gate, w_up, w_down, out_grad):
@@ -77,6 +126,8 @@
     ).astype(jnp.bfloat16)
     returned, grad_back = lax.optimization_barrier((returned, grad_back))
     returned_grad = exchange(grad_back)
+    gain_part = jnp.sum(grad_back.astype(jnp.float32) * arrived.astype(jnp.float32), axis=0)
+    grad_gain = total_over_devices(gain_part) / norm_gain
     grad_down = contract(hidden, arrived_grad, 0, 0).astype(jnp.bfloat16)
     grad_gate = contract(arrived, grad_pre, 0, 0).astype(jnp.bfloat16)
     grad_up = contract(arrived, grad_upval, 0, 0).astype(jnp.bfloat16)
@@ -88,16 +139,7 @@
     )
     grad_probs = jnp.stack([jnp.sum(grad_in * p, axis=1) for p in picked], axis=1)
 
-    grad_normed = contract(chosen, returned_grad, 0, 0)
-    gain_part = jnp.sum(grad_normed * normed, axis=0)
-    parts = exchange(jnp.broadcast_to(gain_part[None, :], (devices_all, width)))
-    grad_gain = jnp.sum(parts, axis=0)
-    grad_scaled = grad_normed * norm_gain
-    grad_tokens = (
-        grad_in
-        + inverse_rms
-        * (grad_scaled - normed * jnp.mean(grad_scaled * normed, axis=1, keepdims=True))
-    ).astype(jnp.bfloat16)
+    grad_tokens = tokens_gradient(chosen, returned_grad, tokens, norm_gain, out_grad)
     return (
         mixed,
         grad_probs,

time: 237 us -> 236 us (level)
  waiting for transfers between devices: 148 us -> 140 us
  matrix products: 55.2 us -> 49.8 us
  starting transfers between devices: 25.4 us -> 30.4 us
  Pallas kernels: 0 us -> 3.62 us
    all_to_all x5 -> x4, waiting for transfers between devices: 148 us -> 114 us  [exchange(): lax.all_to_all(shaped, BOTH, split_axis=0, concat_axis=0, tiled=True)]
    ppermute x0 -> x5, waiting for transfers between devices: none -> 25.7 us  [total_over_devices(): lax.ppermute(part, axis, [(i, i ^ apart) for i in range(size)])]
    ppermute x0 -> x5, starting transfers between devices: none -> 9.56 us  [total_over_devices(): lax.ppermute(part, axis, [(i, i ^ apart) for i in range(size)])]
    dot_general x14 -> x13, matrix products: 55.2 us -> 49.8 us  [contract(): lax.dot_general(left, right, (((left_dim,), (right_dim,)), ((), ())), pre...]
    all_to_all x5 -> x4, starting transfers between devices: 25.4 us -> 20.9 us  [exchange(): lax.all_to_all(shaped, BOTH, split_axis=0, concat_axis=0, tiled=True)]
    pallas_call x0 -> x1, Pallas kernels: none -> 3.62 us  [tokens_gradient(): pl.pallas_call(tokens_gradient_kernel, grid=(rows // step,), out_shape=ja...]
  transfers between devices with their start and end apart: 5 -> 9, of which waited for: 5 -> 6; matrix products, arithmetic and copies ran while one was open for 21% -> 21% of each run, Pallas kernels for 0% -> 0%
where the time goes in v3:
time: 236 us
  waiting for transfers between devices  140 us (59%)
  matrix products  49.8 us (21%)
  starting transfers between devices  30.4 us (13%)
  other arithmetic  6.22 us (3%)
  local copies, waits for them, and re-layouts  4.41 us (2%)
  Pallas kernels  3.62 us (2%)
    all_to_all x4, waiting for transfers between devices, exchange(): lax.all_to_all(shaped, BOTH, split_axis=0, concat_axis=0, tiled=True)  114 us
    dot_general x13, matrix products, contract(): lax.dot_general(left, right, (((left_dim,), (right_dim,)), ((), ())), pre...  49.8 us
    ppermute x5, waiting for transfers between devices, total_over_devices(): lax.ppermute(part, axis, [(i, i ^ apart) for i in range(size)])  25.7 us
    all_to_all x4, starting transfers between devices, exchange(): lax.all_to_all(shaped, BOTH, split_axis=0, concat_axis=0, tiled=True)  20.9 us
    ppermute x5, starting transfers between devices, total_over_devices(): lax.ppermute(part, axis, [(i, i ^ apart) for i in range(size)])  9.56 us
  transfers between devices with their start and end apart: 9, of which 6 were waited for; matrix products, arithmetic and copies ran while one was open for 21% of the time, Pallas kernels for 0%

profile of v3, /device:TPU:0, one launch (start us, length us, event | category | flops | bytes accessed | tf_op | source)
XLA Modules:
  0.0 235.5 jit_solution(5108517576127052326)
XLA Ops:
  0.6 0.0 copy-start
  0.6 1.4 fusion.23
  2.0 0.8 slice_bitcast_fusion.2
  2.8 0.2 add_reduce_fusion.1
  3.0 0.8 multiply_add_fusion.1
  3.7 3.2 %convolution_convert_fusion.3 = bf16[512,2048]{1,0:T(8,128)(2,1)} fusion(bf16[128,2048]{1,0:T(8,128)(2,1)} %tokens_ref.1, f32[2048]{0:T(1024)} %param.11, f32[128]{0:T(128)S(1)} %add_rsqrt_fusion, s32[128]{0:T(128)S(1)} %get-tuple-element.25, s32[128]{0:T(128)S(1)} %get-tuple-element.24), kind=kOutput, calls=%fused_computation.18 | convolution fusion | flops 271056896 | bytes 2631168 | tf_op jit(solution)/shard_map/dot_general | solution.py:12
  6.9 7.4 %all-to-all-start = ((bf16[32,16,2048]{2,1,0:T(8,128)(2,1)}), bf16[32,16,2048]{2,1,0:T(8,128)(2,1)}, u32[]{:S(2)}, u32[]{:S(2)}) async-start(bf16[32,16,2048]{2,1,0:T(8,128)(2,1)} %bitcast.70), calls=%async_computation | async-start | bytes 4194304 | tf_op jit(solution)/shard_map/all_to_all | solution.py:19
  14.3 0.0 copy-done.7
  14.4 0.2 select_reduce_fusion
  14.6 3.1 %multiply_convert_fusion = bf16[512,2048]{1,0:T(8,128)(2,1)} fusion(bf16[128,2048]{1,0:T(8,128)(2,1)} %grad_ref.1, f32[512]{0:T(512)S(1)} %add.82, s32[128]{0:T(128)S(1)} %get-tuple-element.25, s32[128]{0:T(128)S(1)} %get-tuple-element.24), kind=kOutput, calls=%fused_computation.2 | convolution fusion | flops 271056896 | bytes 2624512 | tf_op jit(solution)/shard_map/dot_general | solution.py:12
  17.7 44.2 %all-to-all-done = bf16[32,16,2048]{2,1,0:T(8,128)(2,1)} async-done(((bf16[32,16,2048]{2,1,0:T(8,128)(2,1)}), bf16[32,16,2048]{2,1,0:T(8,128)(2,1)}, u32[]{:S(2)}, u32[]{:S(2)}) %all-to-all-start) | async-done | bytes 2097184 | tf_op jit(solution)/shard_map/all_to_all | solution.py:19
  61.8 4.3 %all-to-all-start.1 = ((bf16[32,16,2048]{2,1,0:T(8,128)(2,1)}), bf16[32,16,2048]{2,1,0:T(8,128)(2,1)}, u32[]{:S(2)}, u32[]{:S(2)}) async-start(bf16[32,16,2048]{2,1,0:T(8,128)(2,1)} %bitcast.71), calls=%async_computation.1 | async-start | bytes 4194304 | tf_op jit(solution)/shard_map/all_to_all | solution.py:19
  66.1 0.0 copy-start.8
  66.1 4.5 %fusion.10 = f32[512,768]{1,0:T(8,128)S(1)} fusion(bf16[512,2048]{1,0:T(8,128)(2,1)} %bitcast.4, bf16[1,2048,768]{2,1,0:T(8,128)(2,1)} %param.12), kind=kOutput, calls=%fused_computation.16 | convolution fusion | flops 1610612736 | bytes 6815744 | tf_op jit(solution)/shard_map/dot_general | solution.py:12
  70.6 0.0 copy-done.8
  70.6 0.0 copy-start.16
  70.6 5.2 %multiply_convert_fusion.3 = (bf16[512,768]{1,0:T(8,128)(2,1)S(1)}, f32[512,768]{1,0:T(8,128)}) fusion(f32[512,768]{1,0:T(8,128)S(1)} %fusion.10, bf16[512,2048]{1,0:T(8,128)(2,1)} %bitcast.4, bf16[1,2048,768]{2,1,0:T(8,128)(2,1)S(1)} %copy-done.8), kind=kOutput, calls=%fused_computation.25 | convolution fusion | flops 1612972032 | bytes 9175040 | tf_op jit(solution)/shard_map/dot_general | solution.py:12
  75.8 0.0 copy-done.16
  75.8 0.9 copy-done.14
  76.7 0.0 copy-done
  76.7 3.2 %fusion.12 = bf16[512,2048]{1,0:T(8,128)(2,1)} fusion(bf16[512,768]{1,0:T(8,128)(2,1)S(1)} %get-tuple-element.28, bf16[1,768,2048]{2,1,0:T(8,128)(2,1)S(1)} %copy-done), kind=kOutput, calls=%fused_computation.19 | convolution fusion | flops 1611661312 | bytes 6029312 | tf_op jit(solution)/shard_map/dot_general | solution.py:12
  79.8 33.6 %all-to-all-done.1 = bf16[32,16,2048]{2,1,0:T(8,128)(2,1)} async-done(((bf16[32,16,2048]{2,1,0:T(8,128)(2,1)}), bf16[32,16,2048]{2,1,0:T(8,128)(2,1)}, u32[]{:S(2)}, u32[]{:S(2)}) %all-to-all-start.1) | async-done | bytes 2097184 | tf_op jit(solution)/shard_map/all_to_all | solution.py:19
  113.4 4.5 %all-to-all-start.2 = ((bf16[32,16,2048]{2,1,0:T(8,128)(2,1)}), bf16[32,16,2048]{2,1,0:T(8,128)(2,1)}, u32[]{:S(2)}, u32[]{:S(2)}) async-start(bf16[32,16,2048]{2,1,0:T(8,128)(2,1)} %bitcast.72), calls=%async_computation.2 | async-start | bytes 4194304 | tf_op jit(solution)/shard_map/all_to_all | solution.py:19
  117.9 0.0 copy-start.9
  117.9 4.9 %multiply_convert_fusion.2 = (bf16[512,768]{1,0:T(8,128)(2,1)S(1)}, bf16[512,768]{1,0:T(8,128)(2,1)S(1)}) fusion(f32[512,768]{1,0:T(8,128)} %copy-done.16, f32[512,768]{1,0:T(8,128)} %get-tuple-element.29, bf16[512,2048]{1,0:T(8,128)(2,1)} %bitcast.10, bf16[1,768,2048]{2,1,0:T(8,128)(2,1)S(1)} %copy-done), kind=kOutput, calls=%fused_computation.24 | convolution fusion | flops 1615724544 | bytes 9961472 | tf_op jit(solution)/shard_map/dot_general | solution.py:12
  122.8 0.0 copy-start.12
  122.8 0.0 copy-start.11
  122.8 0.0 copy-done.9
  122.8 0.0 copy-start.10
  122.8 1.8 fusion.4
  124.7 0.0 copy-done.12
  124.7 0.0 copy-done.11
  124.7 0.6 copy-done.10
  125.3 3.2 %add_convert_fusion = bf16[512,2048]{1,0:T(8,128)(2,1)} fusion(f32[512,2048]{1,0:T(8,128)S(1)} %fusion.4, bf16[512,768]{1,0:T(8,128)(2,1)S(1)} %get-tuple-element.19, bf16[1,2048,768]{2,1,0:T(8,128)(2,1)S(1)} %copy-done.10), kind=kOutput, calls=%fused_computation.1 | convolution fusion | flops 1612709888 | bytes 10223616 | tf_op jit(solution)/shard_map/dot_general | solution.py:12
  128.5 36.7 %all-to-all-done.2 = bf16[32,16,2048]{2,1,0:T(8,128)(2,1)} async-done(((bf16[32,16,2048]{2,1,0:T(8,128)(2,1)}), bf16[32,16,2048]{2,1,0:T(8,128)(2,1)}, u32[]{:S(2)}, u32[]{:S(2)}) %all-to-all-start.2) | async-done | bytes 2097184 | tf_op jit(solution)/shard_map/all_to_all | solution.py:19
  165.2 4.7 %all-to-all-start.3 = ((bf16[32,16,2048]{2,1,0:T(8,128)(2,1)}), bf16[32,16,2048]{2,1,0:T(8,128)(2,1)}, u32[]{:S(2)}, u32[]{:S(2)}) async-start(bf16[32,16,2048]{2,1,0:T(8,128)(2,1)} %bitcast.69), calls=%async_computation.3 | async-start | bytes 4194304 | tf_op jit(solution)/shard_map/all_to_all | solution.py:19
  169.9 0.1 fusion.36.chosen_ref
  170.0 0.0 copy-start.6
  170.0 5.4 %fusion.15 = bf16[1,2048,768]{2,1,0:T(8,128)(2,1)} fusion(bf16[512,2048]{1,0:T(8,128)(2,1)} %bitcast.4, bf16[512,768]{1,0:T(8,128)(2,1)} %copy-done.11), kind=kOutput, calls=%fused_computation.20 | convolution fusion | flops 1612185600 | bytes 6029312 | tf_op jit(solution)/shard_map/dot_general | solution.py:12
  175.4 0.0 copy-done.6
  175.4 2.4 %multiply_reduce_fusion = f32[2048]{0:T(1024)S(1)} fusion(bf16[512,2048]{1,0:T(8,128)(2,1)S(1)} %copy-done.6, bf16[32,16,2048]{2,1,0:T(8,128)(2,1)} %all-to-all-done), kind=kLoop, calls=%fused_computation | loop fusion | flops 4192256 | bytes 4202496 | tf_op jit(solution)/shard_map/reduce_sum | solution.py:129
  177.8 2.1 collective-permute-start
  179.9 0.0 copy-done.13
  179.9 5.1 %fusion.16 = bf16[1,2048,768]{2,1,0:T(8,128)(2,1)} fusion(bf16[512,2048]{1,0:T(8,128)(2,1)} %bitcast.4, bf16[512,768]{1,0:T(8,128)(2,1)S(1)} %copy-done.13), kind=kOutput, calls=%fused_computation.21 | convolution fusion | flops 1612185600 | bytes 6029312 | tf_op jit(solution)/shard_map/dot_general | solution.py:12
  185.0 19.4 %collective-permute-done = f32[2048]{0:T(1024)S(1)} collective-permute-done((f32[2048]{0:T(1024)S(1)}, f32[2048]{0:T(1024)S(1)}, u32[]{:S(2)}, u32[]{:S(2)}) %collective-permute-start) | collective-permute-done | bytes 8224 | tf_op jit(solution)/shard_map/ppermute | solution.py:42
  204.4 4.7 %collective-permute-start.1 = (f32[2048]{0:T(1024)S(1)}, f32[2048]{0:T(1024)S(1)}, u32[]{:S(2)}, u32[]{:S(2)}) collective-permute-start(f32[2048]{0:T(1024)S(1)} %add.87), channel_id=1, source_target_pairs={{0,2},{1,3},{2,0},{3,1},{4,6},{5,7},{6,4},{7,5},{8,10},{9,11},{10,... | collective-permute-start | bytes 24584 | tf_op jit(solution)/shard_map/ppermute | solution.py:42
  209.1 5.1 %fusion.17 = bf16[1,768,2048]{2,1,0:T(8,128)(2,1)} fusion(bf16[512,768]{1,0:T(8,128)(2,1)S(1)} %copy-done.15, bf16[512,2048]{1,0:T(8,128)(2,1)} %bitcast.10), kind=kOutput, calls=%fused_computation.22 | convolution fusion | flops 1612185600 | bytes 6029312 | tf_op jit(solution)/shard_map/dot_general | solution.py:12
  214.2 4.7 %collective-permute-done.1 = f32[2048]{0:T(1024)S(1)} collective-permute-done((f32[2048]{0:T(1024)S(1)}, f32[2048]{0:T(1024)S(1)}, u32[]{:S(2)}, u32[]{:S(2)}) %collective-permute-start.1) | collective-permute-done | bytes 8224 | tf_op jit(solution)/shard_map/ppermute | solution.py:42
  218.8 0.0 collective-permute-start.2
  218.8 2.1 fusion.30
  220.9 0.0 collective-permute-done.2
  221.0 0.0 copy-start.5
  221.0 1.3 collective-permute-start.3
  222.3 0.0 copy-done.3
  222.3 3.3 %fusion.21 = (f32[128]{0:T(128)S(1)}, f32[128]{0:T(128)S(1)}, bf16[128,2048]{1,0:T(8,128)(2,1)}) fusion(bf16[128,2048]{1,0:T(8,128)(2,1)S(1)} %copy-done.3, f32[128,2048]{1,0:T(8,128)S(1)} %fusion.30, f32[128]{0:T(128)S(1)} %get-tuple-element.22, f32[128]{0:T(128)S(1)} %get-tuple-element.23, bf16[128,2048]{1,0:T(8,128)(2,1)S(1)} %copy-done.1, ...), kind=kOutput, calls=%fused_computation.33 | convolution fusion | flops 271384320 | bytes 4721152 | tf_op jit(solution)/shard_map/dot_general | solution.py:12
  225.5 0.0 collective-permute-done.3
  225.5 1.5 collective-permute-start.4
  227.0 0.6 pad_maximum_fusion
  227.6 1.6 collective-permute-done.4
  229.2 0.6 add_divide_fusion.1
  229.8 0.0 all-to-all-done.3
  229.8 1.0 copy-done.2
  230.8 1.0 copy-done.4
  231.9 3.6 %shard_map.135 = bf16[128,2048]{1,0:T(8,128)(2,1)} custom-call(bf16[128,512]{1,0:T(8,128)(2,1)S(1)} %fusion.36.chosen_ref, bf16[512,2048]{1,0:T(8,128)(2,1)} %bitcast.16.back_ref, bf16[128,2048]{1,0:T(8,128)(2,1)S(1)} %copy-done.2, f32[1,2048]{1,0:T(1,128)S(1)} %bitcast.68, bf16[128,2048]{1,0:T(8,128)(2,1)S(1)} %copy-done.4), custom_call_target="tpu_custom_call" | custom-call | flops 268435456 | bytes 3670016 | tf_op jit(solution)/shard_map/pallas_call | solution.py:64
  (18 shorter events, 0.1 us)
Async XLA Ops:
  0.6 76.0 %copy-start = (bf16[1,768,2048]{2,1,0:T(8,128)(2,1)S(1)}, bf16[1,768,2048]{2,1,0:T(8,128)(2,1)}, u32[]{:S(2)}) copy-start(bf16[1,768,2048]{2,1,0:T(8,128)(2,1)} %param.14) | copy-start | bytes 9437188
  6.9 7.4 %copy-start.7 = (f32[128,2]{0,1:T(2,128)S(1)}, f32[128,2]{0,1:T(2,128)}, u32[]{:S(2)}) copy-start(f32[128,2]{0,1:T(2,128)} %param.10) | copy-start | bytes 3076
  6.9 54.9 %all-to-all-start = ((bf16[32,16,2048]{2,1,0:T(8,128)(2,1)}), bf16[32,16,2048]{2,1,0:T(8,128)(2,1)}, u32[]{:S(2)}, u32[]{:S(2)}) async-start(bf16[32,16,2048]{2,1,0:T(8,128)(2,1)} %bitcast.70), calls=%async_computation | async-start | bytes 4194304 | tf_op jit(solution)/shard_map/all_to_all | solution.py:19
  61.8 51.6 %all-to-all-start.1 = ((bf16[32,16,2048]{2,1,0:T(8,128)(2,1)}), bf16[32,16,2048]{2,1,0:T(8,128)(2,1)}, u32[]{:S(2)}, u32[]{:S(2)}) async-start(bf16[32,16,2048]{2,1,0:T(8,128)(2,1)} %bitcast.71), calls=%async_computation.1 | async-start | bytes 4194304 | tf_op jit(solution)/shard_map/all_to_all | solution.py:19
  66.1 4.5 %copy-start.8 = (bf16[1,2048,768]{2,1,0:T(8,128)(2,1)S(1)}, bf16[1,2048,768]{2,1,0:T(8,128)(2,1)}, u32[]{:S(2)}) copy-start(bf16[1,2048,768]{2,1,0:T(8,128)(2,1)} %param.13) | copy-start | bytes 9437188
  70.6 5.2 %copy-start.16 = (f32[512,768]{1,0:T(8,128)}, f32[512,768]{1,0:T(8,128)S(1)}, u32[]{:S(2)}) copy-start(f32[512,768]{1,0:T(8,128)S(1)} %fusion.10) | copy-start | bytes 4718596
  75.8 0.9 copy-start.14
  113.4 51.8 %all-to-all-start.2 = ((bf16[32,16,2048]{2,1,0:T(8,128)(2,1)}), bf16[32,16,2048]{2,1,0:T(8,128)(2,1)}, u32[]{:S(2)}, u32[]{:S(2)}) async-start(bf16[32,16,2048]{2,1,0:T(8,128)(2,1)} %bitcast.72), calls=%async_computation.2 | async-start | bytes 4194304 | tf_op jit(solution)/shard_map/all_to_all | solution.py:19
  117.9 4.9 %copy-start.9 = (bf16[1,2048,768]{2,1,0:T(8,128)(2,1)S(1)}, bf16[1,2048,768]{2,1,0:T(8,128)(2,1)}, u32[]{:S(2)}) copy-start(bf16[1,2048,768]{2,1,0:T(8,128)(2,1)} %param.13) | copy-start | bytes 9437188
  122.8 1.9 copy-start.12
  122.8 1.9 copy-start.11
  122.8 2.4 %copy-start.10 = (bf16[1,2048,768]{2,1,0:T(8,128)(2,1)S(1)}, bf16[1,2048,768]{2,1,0:T(8,128)(2,1)}, u32[]{:S(2)}) copy-start(bf16[1,2048,768]{2,1,0:T(8,128)(2,1)} %param.12) | copy-start | bytes 9437188
  165.2 64.6 %all-to-all-start.3 = ((bf16[32,16,2048]{2,1,0:T(8,128)(2,1)}), bf16[32,16,2048]{2,1,0:T(8,128)(2,1)}, u32[]{:S(2)}, u32[]{:S(2)}) async-start(bf16[32,16,2048]{2,1,0:T(8,128)(2,1)} %bitcast.69), calls=%async_computation.3 | async-start | bytes 4194304 | tf_op jit(solution)/shard_map/all_to_all | solution.py:19
  170.0 5.4 %copy-start.6 = (bf16[512,2048]{1,0:T(8,128)(2,1)S(1)}, bf16[512,2048]{1,0:T(8,128)(2,1)}, u32[]{:S(2)}) copy-start(bf16[512,2048]{1,0:T(8,128)(2,1)} %add_convert_fusion) | copy-start | bytes 6291460
  175.4 4.5 %copy-start.13 = (bf16[512,768]{1,0:T(8,128)(2,1)S(1)}, bf16[512,768]{1,0:T(8,128)(2,1)}, u32[]{:S(2)}) copy-start(bf16[512,768]{1,0:T(8,128)(2,1)} %copy-done.12) | copy-start | bytes 2359300
  177.8 31.3 %copy-start.15 = (bf16[512,768]{1,0:T(8,128)(2,1)S(1)}, bf16[512,768]{1,0:T(8,128)(2,1)}, u32[]{:S(2)}) copy-start(bf16[512,768]{1,0:T(8,128)(2,1)} %copy-done.14) | copy-start | bytes 2359300
  177.8 26.6 %collective-permute-start = (f32[2048]{0:T(1024)S(1)}, f32[2048]{0:T(1024)S(1)}, u32[]{:S(2)}, u32[]{:S(2)}) collective-permute-start(f32[2048]{0:T(1024)S(1)} %multiply_reduce_fusion), channel_id=1, source_target_pairs={{0,1},{1,0},{2,3},{3,2},{4,5},{5,4},{6,7},{7,6},{8,9},{9,8},{10,11... | collective-permute-start | bytes 24584 | tf_op jit(solution)/shard_map/ppermute | solution.py:42
  204.4 14.4 %collective-permute-start.1 = (f32[2048]{0:T(1024)S(1)}, f32[2048]{0:T(1024)S(1)}, u32[]{:S(2)}, u32[]{:S(2)}) collective-permute-start(f32[2048]{0:T(1024)S(1)} %add.87), channel_id=1, source_target_pairs={{0,2},{1,3},{2,0},{3,1},{4,6},{5,7},{6,4},{7,5},{8,10},{9,11},{10,... | collective-permute-start | bytes 24584 | tf_op jit(solution)/shard_map/ppermute | solution.py:42
  214.2 8.1 %copy-start.1 = (bf16[128,2048]{1,0:T(8,128)(2,1)S(1)}, bf16[128,2048]{1,0:T(8,128)(2,1)}, u32[]{:S(2)}) copy-start(bf16[128,2048]{1,0:T(8,128)(2,1)} %tokens_ref.1) | copy-start | bytes 1572868
  214.2 8.1 %copy-start.3 = (bf16[128,2048]{1,0:T(8,128)(2,1)S(1)}, bf16[128,2048]{1,0:T(8,128)(2,1)}, u32[]{:S(2)}) copy-start(bf16[128,2048]{1,0:T(8,128)(2,1)} %grad_ref.1) | copy-start | bytes 1572868
  218.8 2.1 collective-permute-start.2
  221.0 8.2 %copy-start.5 = (f32[2048]{0:T(1024)S(1)}, f32[2048]{0:T(1024)}, u32[]{:S(2)}) copy-start(f32[2048]{0:T(1024)} %param.11) | copy-start | bytes 24580
  221.0 4.6 %collective-permute-start.3 = (f32[2048]{0:T(1024)S(1)}, f32[2048]{0:T(1024)S(1)}, u32[]{:S(2)}, u32[]{:S(2)}) collective-permute-start(f32[2048]{0:T(1024)S(1)} %add.89), channel_id=1, source_target_pairs={{0,8},{4,12},{8,0},{12,4},{16,24},{20,28},{24,16},{28,20},{1,9},{5... | collective-permute-start | bytes 24584 | tf_op jit(solution)/shard_map/ppermute | solution.py:42
  225.5 3.7 %collective-permute-start.4 = (f32[2048]{0:T(1024)S(1)}, f32[2048]{0:T(1024)S(1)}, u32[]{:S(2)}, u32[]{:S(2)}) collective-permute-start(f32[2048]{0:T(1024)S(1)} %add.90), channel_id=1, source_target_pairs={{0,16},{4,20},{8,24},{12,28},{16,0},{20,4},{24,8},{28,12},{1,17},{... | collective-permute-start | bytes 24584 | tf_op jit(solution)/shard_map/ppermute | solution.py:42
  229.8 1.0 copy-start.2
  230.8 1.0 copy-start.4

commit v4 on v3

--- a/solution.py
+++ b/solution.py
@@ -35,12 +35,11 @@
     ]
 
 
-def total_over_devices(part):
-    for axis in reversed(BOTH):
-        size, apart = lax.axis_size(axis), 1
-        while apart < size:
-            part = part + lax.ppermute(part, axis, [(i, i ^ apart) for i in range(size)])
-            apart *= 2
+def total_over(part, axis):
+    size, apart = lax.axis_size(axis), 1
+    while apart < size:
+        part = part + lax.ppermute(part, axis, [(i, i ^ apart) for i in range(size)])
+        apart *= 2
     return part
 
 
@@ -73,7 +72,7 @@
             own,
         ],
         out_specs=own,
-        compiler_params=pltpu.CompilerParams(vmem_limit_bytes=24 * 2**20),
+        compiler_params=pltpu.CompilerParams(vmem_limit_bytes=56 * 2**20),
         cost_estimate=pl.CostEstimate(
             flops=2 * rows * slots * width,
             bytes_accessed=2 * width * (slots + 3 * rows),
@@ -124,10 +123,11 @@
     grad_back = (
         contract(grad_pre, gate_matrix, 1, 1) + contract(grad_upval, up_matrix, 1, 1)
     ).astype(jnp.bfloat16)
-    returned, grad_back = lax.optimization_barrier((returned, grad_back))
+    gain_part = jnp.sum(grad_back.astype(jnp.float32) * arrived.astype(jnp.float32), axis=0)
+    gain_part = total_over(gain_part, "expert")
+    returned, grad_back, gain_part = lax.optimization_barrier((returned, grad_back, gain_part))
     returned_grad = exchange(grad_back)
-    gain_part = jnp.sum(grad_back.astype(jnp.float32) * arrived.astype(jnp.float32), axis=0)
-    grad_gain = total_over_devices(gain_part) / norm_gain
+    grad_gain = total_over(gain_part, "dp") / norm_gain
     grad_down = contract(hidden, arrived_grad, 0, 0).astype(jnp.bfloat16)
     grad_gate = contract(arrived, grad_pre, 0, 0).astype(jnp.bfloat16)
     grad_up = contract(arrived, grad_upval, 0, 0).astype(jnp.bfloat16)

time: 236 us -> 224 us (0.949)
  waiting for transfers between devices: 140 us -> 129 us
    all_to_all x4, waiting for transfers between devices: 114 us -> 104 us  [exchange(): lax.all_to_all(shaped, BOTH, split_axis=0, concat_axis=0, tiled=True)]
  transfers between devices with their start and end apart: 9 -> 9, of which waited for: 6 -> 8; matrix products, arithmetic and copies ran while one was open for 21% -> 23% of each run, Pallas kernels for 0% -> 0%
where the time goes in v4:
time: 224 us; the launch traced here: 223 us
  waiting for transfers between devices  129 us (58%)
  matrix products  51.6 us (23%)
  starting transfers between devices  30.9 us (14%)
  other arithmetic  4.52 us (2%)
  Pallas kernels  3.95 us (2%)
  local copies, waits for them, and re-layouts  2.31 us (1%)
    all_to_all x4, waiting for transfers between devices, exchange(): lax.all_to_all(shaped, BOTH, split_axis=0, concat_axis=0, tiled=True)  104 us
    dot_general x13, matrix products, contract(): lax.dot_general(left, right, (((left_dim,), (right_dim,)), ((), ())), pre...  51.6 us
    ppermute x5, waiting for transfers between devices, total_over(): lax.ppermute(part, axis, [(i, i ^ apart) for i in range(size)])  25.3 us
    all_to_all x4, starting transfers between devices, exchange(): lax.all_to_all(shaped, BOTH, split_axis=0, concat_axis=0, tiled=True)  20.6 us
    ppermute x5, starting transfers between devices, total_over(): lax.ppermute(part, axis, [(i, i ^ apart) for i in range(size)])  10.2 us
  transfers between devices with their start and end apart: 9, of which 8 were waited for; matrix products, arithmetic and copies ran while one was open for 23% of the time, Pallas kernels for 0%

profile of v4, /device:TPU:0, one launch (start us, length us, event | category | flops | bytes accessed | tf_op | source)
XLA Modules:
  0.0 223.4 jit_solution(12844713110240853462)
XLA Ops:
  0.6 0.0 copy-start
  0.6 1.4 fusion.23
  2.0 0.8 slice_bitcast_fusion.2
  2.8 0.2 add_reduce_fusion.1
  3.0 0.8 multiply_add_fusion.1
  3.7 3.2 %convolution_convert_fusion.3 = bf16[512,2048]{1,0:T(8,128)(2,1)} fusion(bf16[128,2048]{1,0:T(8,128)(2,1)} %tokens_ref.1, f32[2048]{0:T(1024)} %param.11, f32[128]{0:T(128)S(1)} %add_rsqrt_fusion, s32[128]{0:T(128)S(1)} %get-tuple-element.27, s32[128]{0:T(128)S(1)} %get-tuple-element.26), kind=kOutput, calls=%fused_computation.18 | convolution fusion | flops 271056896 | bytes 2631168 | tf_op jit(solution)/shard_map/dot_general | solution.py:12
  6.9 0.0 copy-start.6
  6.9 7.4 %all-to-all-start = ((bf16[32,16,2048]{2,1,0:T(8,128)(2,1)}), bf16[32,16,2048]{2,1,0:T(8,128)(2,1)}, u32[]{:S(2)}, u32[]{:S(2)}) async-start(bf16[32,16,2048]{2,1,0:T(8,128)(2,1)} %bitcast.70), calls=%async_computation | async-start | bytes 4194304 | tf_op jit(solution)/shard_map/all_to_all | solution.py:19
  14.3 0.0 copy-done.6
  14.4 0.2 select_reduce_fusion
  14.6 3.1 %multiply_convert_fusion = bf16[512,2048]{1,0:T(8,128)(2,1)} fusion(bf16[128,2048]{1,0:T(8,128)(2,1)} %grad_ref.1, f32[512]{0:T(512)S(1)} %add.82, s32[128]{0:T(128)S(1)} %get-tuple-element.27, s32[128]{0:T(128)S(1)} %get-tuple-element.26), kind=kOutput, calls=%fused_computation.2 | convolution fusion | flops 271056896 | bytes 2624512 | tf_op jit(solution)/shard_map/dot_general | solution.py:12
  17.7 44.2 %all-to-all-done = bf16[32,16,2048]{2,1,0:T(8,128)(2,1)} async-done(((bf16[32,16,2048]{2,1,0:T(8,128)(2,1)}), bf16[32,16,2048]{2,1,0:T(8,128)(2,1)}, u32[]{:S(2)}, u32[]{:S(2)}) %all-to-all-start) | async-done | bytes 2097184 | tf_op jit(solution)/shard_map/all_to_all | solution.py:19
  61.8 4.3 %all-to-all-start.1 = ((bf16[32,16,2048]{2,1,0:T(8,128)(2,1)}), bf16[32,16,2048]{2,1,0:T(8,128)(2,1)}, u32[]{:S(2)}, u32[]{:S(2)}) async-start(bf16[32,16,2048]{2,1,0:T(8,128)(2,1)} %bitcast.71), calls=%async_computation.1 | async-start | bytes 4194304 | tf_op jit(solution)/shard_map/all_to_all | solution.py:19
  66.1 0.0 copy-start.7
  66.1 4.5 %fusion.10 = f32[512,768]{1,0:T(8,128)S(1)} fusion(bf16[512,2048]{1,0:T(8,128)(2,1)} %bitcast.4, bf16[1,2048,768]{2,1,0:T(8,128)(2,1)} %param.12), kind=kOutput, calls=%fused_computation.16 | convolution fusion | flops 1610612736 | bytes 6815744 | tf_op jit(solution)/shard_map/dot_general | solution.py:12
  70.6 0.0 copy-done.7
  70.6 0.0 copy-start.13
  70.6 5.2 %multiply_convert_fusion.3 = (bf16[512,768]{1,0:T(8,128)(2,1)S(1)}, f32[512,768]{1,0:T(8,128)}) fusion(f32[512,768]{1,0:T(8,128)S(1)} %fusion.10, bf16[512,2048]{1,0:T(8,128)(2,1)} %bitcast.4, bf16[1,2048,768]{2,1,0:T(8,128)(2,1)S(1)} %copy-done.7), kind=kOutput, calls=%fused_computation.25 | convolution fusion | flops 1612972032 | bytes 9175040 | tf_op jit(solution)/shard_map/dot_general | solution.py:12
  75.8 0.0 copy-done.13
  75.8 0.0 copy-start.11
  75.8 0.9 copy-done.11
  76.7 0.0 copy-done
  76.7 3.2 %fusion.12 = bf16[512,2048]{1,0:T(8,128)(2,1)} fusion(bf16[512,768]{1,0:T(8,128)(2,1)S(1)} %get-tuple-element.30, bf16[1,768,2048]{2,1,0:T(8,128)(2,1)S(1)} %copy-done), kind=kOutput, calls=%fused_computation.19 | convolution fusion | flops 1611661312 | bytes 6029312 | tf_op jit(solution)/shard_map/dot_general | solution.py:12
  79.8 33.6 %all-to-all-done.1 = bf16[32,16,2048]{2,1,0:T(8,128)(2,1)} async-done(((bf16[32,16,2048]{2,1,0:T(8,128)(2,1)}), bf16[32,16,2048]{2,1,0:T(8,128)(2,1)}, u32[]{:S(2)}, u32[]{:S(2)}) %all-to-all-start.1) | async-done | bytes 2097184 | tf_op jit(solution)/shard_map/all_to_all | solution.py:19
  113.4 4.5 %all-to-all-start.2 = ((bf16[32,16,2048]{2,1,0:T(8,128)(2,1)}), bf16[32,16,2048]{2,1,0:T(8,128)(2,1)}, u32[]{:S(2)}, u32[]{:S(2)}) async-start(bf16[32,16,2048]{2,1,0:T(8,128)(2,1)} %bitcast.73), calls=%async_computation.2 | async-start | bytes 4194304 | tf_op jit(solution)/shard_map/all_to_all | solution.py:19
  117.9 0.0 copy-start.8
  117.9 4.9 %multiply_convert_fusion.2 = (bf16[512,768]{1,0:T(8,128)(2,1)S(1)}, bf16[512,768]{1,0:T(8,128)(2,1)S(1)}) fusion(f32[512,768]{1,0:T(8,128)} %copy-done.13, f32[512,768]{1,0:T(8,128)} %get-tuple-element.31, bf16[512,2048]{1,0:T(8,128)(2,1)} %bitcast.10, bf16[1,768,2048]{2,1,0:T(8,128)(2,1)S(1)} %copy-done), kind=kOutput, calls=%fused_computation.24 | convolution fusion | flops 1615724544 | bytes 9961472 | tf_op jit(solution)/shard_map/dot_general | solution.py:12
  122.8 0.0 copy-start.9
  122.8 0.0 copy-start.4
  122.8 0.0 copy-done.8
  122.8 0.0 copy-start.3
  122.8 1.8 fusion.4
  124.7 0.0 copy-done.9
  124.7 0.0 copy-done.4
  124.7 0.6 copy-done.3
  125.3 4.9 %multiply_reduce_fusion = (f32[2048]{0:T(1024)S(1)}, bf16[512,2048]{1,0:T(8,128)(2,1)}) fusion(bf16[32,16,2048]{2,1,0:T(8,128)(2,1)} %all-to-all-done, f32[512,2048]{1,0:T(8,128)S(1)} %fusion.4, bf16[512,768]{1,0:T(8,128)(2,1)S(1)} %get-tuple-element.21, bf16[1,2048,768]{2,1,0:T(8,128)(2,1)S(1)} %copy-done.3), kind=kOutput, calls=%fused_computation | convolution fusion | flops 1616902144 | bytes 12328960 | tf_op jit(solution)/shard_map/dot_general | solution.py:12
  130.2 0.2 collective-permute-start
  130.4 1.0 collective-permute-done
  131.4 1.8 collective-permute-start.1
  133.1 2.1 collective-permute-done.1
  135.3 1.6 collective-permute-start.2
  136.9 2.1 collective-permute-done.2
  138.9 26.3 %all-to-all-done.2 = bf16[32,16,2048]{2,1,0:T(8,128)(2,1)} async-done(((bf16[32,16,2048]{2,1,0:T(8,128)(2,1)}), bf16[32,16,2048]{2,1,0:T(8,128)(2,1)}, u32[]{:S(2)}, u32[]{:S(2)}) %all-to-all-start.2) | async-done | bytes 2097184 | tf_op jit(solution)/shard_map/all_to_all | solution.py:19
  165.2 4.5 %all-to-all-start.3 = ((bf16[32,16,2048]{2,1,0:T(8,128)(2,1)}), bf16[32,16,2048]{2,1,0:T(8,128)(2,1)}, u32[]{:S(2)}, u32[]{:S(2)}) async-start(bf16[32,16,2048]{2,1,0:T(8,128)(2,1)} %bitcast.72), calls=%async_computation.3 | async-start | bytes 4194304 | tf_op jit(solution)/shard_map/all_to_all | solution.py:19
  169.7 0.8 fusion.36.chosen_ref
  170.4 5.3 %fusion.15 = bf16[1,2048,768]{2,1,0:T(8,128)(2,1)} fusion(bf16[512,2048]{1,0:T(8,128)(2,1)} %bitcast.4, bf16[512,768]{1,0:T(8,128)(2,1)} %copy-done.4), kind=kOutput, calls=%fused_computation.20 | convolution fusion | flops 1612185600 | bytes 6029312 | tf_op jit(solution)/shard_map/dot_general | solution.py:12
  175.8 0.0 copy-done.10
  175.8 5.2 %fusion.16 = bf16[1,2048,768]{2,1,0:T(8,128)(2,1)} fusion(bf16[512,2048]{1,0:T(8,128)(2,1)} %bitcast.4, bf16[512,768]{1,0:T(8,128)(2,1)S(1)} %copy-done.10), kind=kOutput, calls=%fused_computation.21 | convolution fusion | flops 1612185600 | bytes 6029312 | tf_op jit(solution)/shard_map/dot_general | solution.py:12
  181.0 0.0 copy-done.12
  181.0 5.1 %fusion.17 = bf16[1,768,2048]{2,1,0:T(8,128)(2,1)} fusion(bf16[512,768]{1,0:T(8,128)(2,1)S(1)} %copy-done.12, bf16[512,2048]{1,0:T(8,128)(2,1)} %bitcast.10), kind=kOutput, calls=%fused_computation.22 | convolution fusion | flops 1612185600 | bytes 6029312 | tf_op jit(solution)/shard_map/dot_general | solution.py:12
  186.1 2.2 collective-permute-start.3
  188.3 2.1 fusion.30
  190.4 0.0 copy-done.1
  190.4 0.0 copy-done.2
  190.4 0.0 copy-start.5
  190.4 3.3 %fusion.21 = (f32[128]{0:T(128)S(1)}, f32[128]{0:T(128)S(1)}, bf16[128,2048]{1,0:T(8,128)(2,1)}) fusion(bf16[128,2048]{1,0:T(8,128)(2,1)S(1)} %copy-done.2, f32[128,2048]{1,0:T(8,128)S(1)} %fusion.30, f32[128]{0:T(128)S(1)} %get-tuple-element.24, f32[128]{0:T(128)S(1)} %get-tuple-element.25, bf16[128,2048]{1,0:T(8,128)(2,1)S(1)} %copy-done.1, ...), kind=kOutput, calls=%fused_computation.33 | convolution fusion | flops 271384320 | bytes 4721152 | tf_op jit(solution)/shard_map/dot_general | solution.py:12
  193.7 10.9 %collective-permute-done.3 = f32[2048]{0:T(1024)S(1)} collective-permute-done((f32[2048]{0:T(1024)S(1)}, f32[2048]{0:T(1024)S(1)}, u32[]{:S(2)}, u32[]{:S(2)}) %collective-permute-start.3) | collective-permute-done | bytes 8224 | tf_op jit(solution)/shard_map/ppermute | solution.py:41
  204.6 4.5 %collective-permute-start.4 = (f32[2048]{0:T(1024)S(1)}, f32[2048]{0:T(1024)S(1)}, u32[]{:S(2)}, u32[]{:S(2)}) collective-permute-start(f32[2048]{0:T(1024)S(1)} %add.90), channel_id=1, source_target_pairs={{0,2},{1,3},{2,0},{3,1},{4,6},{5,7},{6,4},{7,5},{8,10},{9,11},{10,... | collective-permute-start | bytes 24584 | tf_op jit(solution)/shard_map/ppermute | solution.py:41
  209.1 0.6 pad_maximum_fusion
  209.6 9.2 %collective-permute-done.4 = f32[2048]{0:T(1024)S(1)} collective-permute-done((f32[2048]{0:T(1024)S(1)}, f32[2048]{0:T(1024)S(1)}, u32[]{:S(2)}, u32[]{:S(2)}) %collective-permute-start.4) | collective-permute-done | bytes 8224 | tf_op jit(solution)/shard_map/ppermute | solution.py:41
  218.8 0.0 copy-done.5
  218.8 0.6 add_divide_fusion.1
  219.4 0.0 all-to-all-done.3
  219.5 3.9 %shard_map.135 = bf16[128,2048]{1,0:T(8,128)(2,1)} custom-call(bf16[128,512]{1,0:T(8,128)(2,1)} %fusion.36.chosen_ref, bf16[512,2048]{1,0:T(8,128)(2,1)} %bitcast.16.back_ref, bf16[128,2048]{1,0:T(8,128)(2,1)} %tokens_ref.1, f32[1,2048]{1,0:T(1,128)} %bitcast.74, bf16[128,2048]{1,0:T(8,128)(2,1)} %grad_ref.1), custom_call_target="tpu_custom_call" | custom-call | flops 268435456 | bytes 3670016 | tf_op jit(solution)/shard_map/pallas_call | solution.py:63
  (11 shorter events, 0.0 us)
Async XLA Ops:
  0.6 76.0 %copy-start = (bf16[1,768,2048]{2,1,0:T(8,128)(2,1)S(1)}, bf16[1,768,2048]{2,1,0:T(8,128)(2,1)}, u32[]{:S(2)}) copy-start(bf16[1,768,2048]{2,1,0:T(8,128)(2,1)} %param.14) | copy-start | bytes 9437188
  6.9 7.4 %copy-start.6 = (f32[128,2]{0,1:T(2,128)S(1)}, f32[128,2]{0,1:T(2,128)}, u32[]{:S(2)}) copy-start(f32[128,2]{0,1:T(2,128)} %param.10) | copy-start | bytes 3076
  6.9 54.9 %all-to-all-start = ((bf16[32,16,2048]{2,1,0:T(8,128)(2,1)}), bf16[32,16,2048]{2,1,0:T(8,128)(2,1)}, u32[]{:S(2)}, u32[]{:S(2)}) async-start(bf16[32,16,2048]{2,1,0:T(8,128)(2,1)} %bitcast.70), calls=%async_computation | async-start | bytes 4194304 | tf_op jit(solution)/shard_map/all_to_all | solution.py:19
  61.8 51.6 %all-to-all-start.1 = ((bf16[32,16,2048]{2,1,0:T(8,128)(2,1)}), bf16[32,16,2048]{2,1,0:T(8,128)(2,1)}, u32[]{:S(2)}, u32[]{:S(2)}) async-start(bf16[32,16,2048]{2,1,0:T(8,128)(2,1)} %bitcast.71), calls=%async_computation.1 | async-start | bytes 4194304 | tf_op jit(solution)/shard_map/all_to_all | solution.py:19
  66.1 4.5 %copy-start.7 = (bf16[1,2048,768]{2,1,0:T(8,128)(2,1)S(1)}, bf16[1,2048,768]{2,1,0:T(8,128)(2,1)}, u32[]{:S(2)}) copy-start(bf16[1,2048,768]{2,1,0:T(8,128)(2,1)} %param.13) | copy-start | bytes 9437188
  70.6 5.2 %copy-start.13 = (f32[512,768]{1,0:T(8,128)}, f32[512,768]{1,0:T(8,128)S(1)}, u32[]{:S(2)}) copy-start(f32[512,768]{1,0:T(8,128)S(1)} %fusion.10) | copy-start | bytes 4718596
  75.8 0.9 copy-start.11
  113.4 51.8 %all-to-all-start.2 = ((bf16[32,16,2048]{2,1,0:T(8,128)(2,1)}), bf16[32,16,2048]{2,1,0:T(8,128)(2,1)}, u32[]{:S(2)}, u32[]{:S(2)}) async-start(bf16[32,16,2048]{2,1,0:T(8,128)(2,1)} %bitcast.73), calls=%async_computation.2 | async-start | bytes 4194304 | tf_op jit(solution)/shard_map/all_to_all | solution.py:19
  117.9 4.9 %copy-start.8 = (bf16[1,2048,768]{2,1,0:T(8,128)(2,1)S(1)}, bf16[1,2048,768]{2,1,0:T(8,128)(2,1)}, u32[]{:S(2)}) copy-start(bf16[1,2048,768]{2,1,0:T(8,128)(2,1)} %param.13) | copy-start | bytes 9437188
  122.8 1.9 copy-start.9
  122.8 1.9 copy-start.4
  122.8 2.4 %copy-start.3 = (bf16[1,2048,768]{2,1,0:T(8,128)(2,1)S(1)}, bf16[1,2048,768]{2,1,0:T(8,128)(2,1)}, u32[]{:S(2)}) copy-start(bf16[1,2048,768]{2,1,0:T(8,128)(2,1)} %param.12) | copy-start | bytes 9437188
  130.2 1.2 collective-permute-start
  131.4 3.9 %collective-permute-start.1 = (f32[2048]{0:T(1024)S(1)}, f32[2048]{0:T(1024)S(1)}, u32[]{:S(2)}, u32[]{:S(2)}) collective-permute-start(f32[2048]{0:T(1024)S(1)} %add.85), channel_id=1, source_target_pairs={{0,8},{4,12},{8,0},{12,4},{16,24},{20,28},{24,16},{28,20},{1,9},{5... | collective-permute-start | bytes 24584 | tf_op jit(solution)/shard_map/ppermute | solution.py:41
  135.3 3.7 %collective-permute-start.2 = (f32[2048]{0:T(1024)S(1)}, f32[2048]{0:T(1024)S(1)}, u32[]{:S(2)}, u32[]{:S(2)}) collective-permute-start(f32[2048]{0:T(1024)S(1)} %add.86), channel_id=1, source_target_pairs={{0,16},{4,20},{8,24},{12,28},{16,0},{20,4},{24,8},{28,12},{1,17},{... | collective-permute-start | bytes 24584 | tf_op jit(solution)/shard_map/ppermute | solution.py:41
  165.2 54.2 %all-to-all-start.3 = ((bf16[32,16,2048]{2,1,0:T(8,128)(2,1)}), bf16[32,16,2048]{2,1,0:T(8,128)(2,1)}, u32[]{:S(2)}, u32[]{:S(2)}) async-start(bf16[32,16,2048]{2,1,0:T(8,128)(2,1)} %bitcast.72), calls=%async_computation.3 | async-start | bytes 4194304 | tf_op jit(solution)/shard_map/all_to_all | solution.py:19
  170.4 5.3 %copy-start.10 = (bf16[512,768]{1,0:T(8,128)(2,1)S(1)}, bf16[512,768]{1,0:T(8,128)(2,1)}, u32[]{:S(2)}) copy-start(bf16[512,768]{1,0:T(8,128)(2,1)} %copy-done.9) | copy-start | bytes 2359300
  175.8 5.2 %copy-start.12 = (bf16[512,768]{1,0:T(8,128)(2,1)S(1)}, bf16[512,768]{1,0:T(8,128)(2,1)}, u32[]{:S(2)}) copy-start(bf16[512,768]{1,0:T(8,128)(2,1)} %copy-done.11) | copy-start | bytes 2359300
  186.1 4.3 %copy-start.1 = (bf16[128,2048]{1,0:T(8,128)(2,1)S(1)}, bf16[128,2048]{1,0:T(8,128)(2,1)}, u32[]{:S(2)}) copy-start(bf16[128,2048]{1,0:T(8,128)(2,1)} %tokens_ref.1) | copy-start | bytes 1572868
  186.1 4.3 %copy-start.2 = (bf16[128,2048]{1,0:T(8,128)(2,1)S(1)}, bf16[128,2048]{1,0:T(8,128)(2,1)}, u32[]{:S(2)}) copy-start(bf16[128,2048]{1,0:T(8,128)(2,1)} %grad_ref.1) | copy-start | bytes 1572868
  186.1 18.5 %collective-permute-start.3 = (f32[2048]{0:T(1024)S(1)}, f32[2048]{0:T(1024)S(1)}, u32[]{:S(2)}, u32[]{:S(2)}) collective-permute-start(f32[2048]{0:T(1024)S(1)} %add.87), channel_id=1, source_target_pairs={{0,1},{1,0},{2,3},{3,2},{4,5},{5,4},{6,7},{7,6},{8,9},{9,8},{10,11... | collective-permute-start | bytes 24584 | tf_op jit(solution)/shard_map/ppermute | solution.py:41
  190.4 28.4 %copy-start.5 = (f32[2048]{0:T(1024)S(1)}, f32[2048]{0:T(1024)}, u32[]{:S(2)}) copy-start(f32[2048]{0:T(1024)} %param.11) | copy-start | bytes 24580
  204.6 14.3 %collective-permute-start.4 = (f32[2048]{0:T(1024)S(1)}, f32[2048]{0:T(1024)S(1)}, u32[]{:S(2)}, u32[]{:S(2)}) collective-permute-start(f32[2048]{0:T(1024)S(1)} %add.90), channel_id=1, source_target_pairs={{0,2},{1,3},{2,0},{3,1},{4,6},{5,7},{6,4},{7,5},{8,10},{9,11},{10,... | collective-permute-start | bytes 24584 | tf_op jit(solution)/shard_map/ppermute | solution.py:41
